TPU v7x, 512 devices: a whole 4x4x16 slice. The times are simulated.
512 devices in a mesh: gx: 16 (over z), gz: 32 (over y, x, core).
Axes of the slice: x: 4, y: 4, z: 16, core: 2. Of those that a mesh axis runs over, the one named last changes fastest.
Arguments:
- velocity: float32 [3, 4, 2048, 2048], P(None, None, 'gz', 'gx'), may hold values from -6 to 6
- old_rhs: float32 [3, 4, 2048, 2048], P(None, None, 'gz', 'gx'), may hold values from -6 to 6
Outputs:
- new_velocity: float32 [3, 4, 2048, 2048], P(None, None, 'gz', 'gx')
- rhs: float32 [3, 4, 2048, 2048], P(None, None, 'gz', 'gx')
All inputs are finite; a program needn't handle non-finite values.
Results may differ from a plain program's by a relative error of at most 0.0001.
Values sent between devices are 32-bit elements; how exact they have to be, the bound alone decides.
No kernel may reach another device: no remote copies, remote signals or barrier semaphores. Data moves between devices by JAX's collectives and lax.ppermute only.
A program may use at most 64 MiB of HBM per device.

v0:
```python
import math

import jax
import jax.numpy as jnp
from jax import lax
from jax.sharding import PartitionSpec as P

first_alpha = 1.0 / 3.0
first_near = 14.0 / 9.0
first_far = 1.0 / 9.0
second_alpha = 2.0 / 11.0
second_near = 12.0 / 11.0
second_far = 3.0 / 11.0
viscosity = 0.2
time_step = 0.25
gamma_now = 5.0 / 12.0
zeta_old = -17.0 / 60.0
first_stencil = (
    (1, 0.5 * first_near),
    (-1, -0.5 * first_near),
    (2, 0.25 * first_far),
    (-2, -0.25 * first_far),
)
second_stencil = (
    (0, -2.0 * second_near - 0.5 * second_far),
    (1, second_near),
    (-1, second_near),
    (2, 0.25 * second_far),
    (-2, 0.25 * second_far),
)


def padded_2(cells, sides, width):
    for axis, dim in sides:
        count = lax.axis_size(axis)
        head = lax.slice_in_dim(cells, 0, width, axis=dim)
        tail = lax.slice_in_dim(cells, cells.shape[dim] - width, cells.shape[dim], axis=dim)
        cells = jnp.concatenate(
            [
                lax.ppermute(tail, axis, [(i, (i + 1) % count) for i in range(count)]),
                cells,
                lax.ppermute(head, axis, [((i + 1) % count, i) for i in range(count)]),
            ],
            axis=dim,
        )
    return cells


def decay_power(distance, off_diag):
    root_value = (-1.0 + math.sqrt(1.0 - 4.0 * off_diag * off_diag)) / (2.0 * off_diag)
    lead_factor = 1.0 / (1.0 + 2.0 * off_diag * root_value)
    magnitude = jnp.exp(distance.astype(jnp.float32) * math.log(-root_value))
    parity = (1 - 2 * (distance % 2)).astype(jnp.float32)
    return lead_factor * parity * magnitude


def line_matrix(stencil, off_diag, extent):
    row_ids = lax.broadcasted_iota(jnp.int32, (extent, 3 * extent), 0)
    column_ids = lax.broadcasted_iota(jnp.int32, (extent, 3 * extent), 1)
    total = jnp.zeros((extent, 3 * extent), jnp.float32)
    for offset, weight in stencil:
        total = total + weight * decay_power(
            jnp.abs(column_ids - extent - row_ids + offset), off_diag
        )
    return total


def apply_matrix(values_in, matrix):
    flattened = values_in.reshape(-1, values_in.shape[-1])
    product = jnp.dot(
        flattened, matrix, precision=lax.Precision.HIGHEST, preferred_element_type=jnp.float32
    )
    return product.reshape(values_in.shape[:-1] + (matrix.shape[1],))


def line_solve(fields, stencil, off_diag, extent):
    shape_in = fields.shape
    blocks = fields.reshape(shape_in[:-1] + (shape_in[-1] // extent, extent))
    spread = apply_matrix(blocks, line_matrix(stencil, off_diag, extent))
    result = (
        spread[..., extent : 2 * extent]
        + jnp.roll(spread[..., :extent], -1, axis=-2)
        + jnp.roll(spread[..., 2 * extent :], 1, axis=-2)
    )
    return result.reshape(shape_in)


def stream_terms(stream_vel, slopes):
    return -0.5 * (stream_vel * slopes[0:3] + slopes[3:6]) + viscosity * slopes[6:9]


def span_shifted(padded, offset, extent):
    return lax.slice_in_dim(padded, 3 + offset, 3 + offset + extent, axis=2)


def span_first(padded, extent):
    return (
        45.0 * (span_shifted(padded, 1, extent) - span_shifted(padded, -1, extent))
        - 9.0 * (span_shifted(padded, 2, extent) - span_shifted(padded, -2, extent))
        + (span_shifted(padded, 3, extent) - span_shifted(padded, -3, extent))
    ) / 60.0


def span_second(padded, extent):
    return (
        2.0 * (span_shifted(padded, 3, extent) + span_shifted(padded, -3, extent))
        - 27.0 * (span_shifted(padded, 2, extent) + span_shifted(padded, -2, extent))
        + 270.0 * (span_shifted(padded, 1, extent) + span_shifted(padded, -1, extent))
        - 490.0 * span_shifted(padded, 0, extent)
    ) / 180.0


def local(velocity, old_rhs):
    span_cells = velocity.shape[2]
    stream_cells = velocity.shape[3]
    span_padded = padded_2(velocity, (("gz", 2),), 3)
    span_flux = span_padded[2][None] * span_padded
    span_slopes = span_first(jnp.concatenate([span_padded, span_flux], 0), span_cells)
    span_curves = span_second(span_padded, span_cells)
    stream_vel = velocity[0][None]
    span_vel = velocity[2][None]
    full_lines = lax.all_to_all(velocity, "gx", split_axis=2, concat_axis=3, tiled=True)
    flux_terms = full_lines[0][None] * full_lines
    fields = jnp.concatenate([full_lines, flux_terms], 0)
    slope_part = line_solve(fields, first_stencil, first_alpha, stream_cells)
    curve_part = line_solve(full_lines, second_stencil, second_alpha, stream_cells)
    result = jnp.concatenate([slope_part, curve_part], 0)
    returned = lax.all_to_all(result, "gx", split_axis=3, concat_axis=2, tiled=True)
    stream_part = stream_terms(stream_vel, returned)
    right_side = (
        stream_part
        - 0.5 * (span_vel * span_slopes[0:3] + span_slopes[3:6])
        + viscosity * span_curves
    )
    new_velocity = velocity + time_step * (gamma_now * right_side + zeta_old * old_rhs)
    return (new_velocity, right_side)


def solution(mesh):
    return jax.shard_map(
        local,
        mesh=mesh,
        in_specs=(P(None, None, "gz", "gx"), P(None, None, "gz", "gx")),
        out_specs=(P(None, None, "gz", "gx"), P(None, None, "gz", "gx")),
        check_vma=False,
    )
```

profile of v0, /device:TPU:6, one launch (start us, length us, event | category | flops | bytes accessed | tf_op | source)
XLA Modules:
  0.0 197.1 jit_solution(6710478932422704053)
XLA Ops:
  0.6 2.0 %copy.32 = f32[3,4,64,128]{3,1,0,2:T(4,128)} copy(f32[3,4,64,128]{3,2,1,0:T(8,128)} %param.2) | data formatting | bytes 786432 | tf_op args[0]
  2.6 15.2 %all-to-all-start = ((f32[3,4,64,128]{3,1,0,2:T(4,128)}), f32[3,4,64,128]{3,1,0,2:T(4,128)S(1)}, u32[]{:S(2)}, u32[]{:S(2)}) async-start(f32[3,4,64,128]{3,1,0,2:T(4,128)} %copy.32), calls=%async_computation | async-start | bytes 786432 | tf_op jit(solution)/shard_map/all_to_all | solution.py:122
  17.8 23.8 %all-to-all-done = f32[3,4,64,128]{3,1,0,2:T(4,128)S(1)} async-done(((f32[3,4,64,128]{3,1,0,2:T(4,128)}), f32[3,4,64,128]{3,1,0,2:T(4,128)S(1)}, u32[]{:S(2)}, u32[]{:S(2)}) %all-to-all-start) | async-done | bytes 393248 | tf_op jit(solution)/shard_map/all_to_all | solution.py:122
  41.6 0.1 copy.48
  41.8 0.1 broadcast_multiply_fusion.1
  41.9 2.7 %fusion.6 = f32[6,4,4,16,384]{4,3,2,1,0:T(8,128)S(1)} fusion(f32[3,4,4,16,128]{4,3,2,1,0:T(8,128)S(1)} %broadcast_multiply_fusion.1, f32[3,4,4,16,128]{4,3,2,1,0:T(8,128)S(1)} %bitcast.47, s32[384]{0:T(512)S(1)} %iota_add_fusion), kind=kOutput, calls=%fused_computation.13 | convolution fusion | flops 910491648 | bytes 3147264 | tf_op jit(solution)/shard_map/dot_general | solution.py:70
  44.6 0.0 copy-start.2
  44.6 0.2 fusion.168
  44.8 1.3 copy-done.2
  46.0 0.7 fusion.167
  46.7 3.0 %convolution_bitcast_fusion = f32[768,384]{0,1:T(8,128)} fusion(f32[768,128]{1,0:T(8,128)S(1)} %bitcast.48, s32[384]{0:T(512)S(1)} %iota_add_fusion), kind=kOutput, calls=%fused_computation | convolution fusion | flops 458342400 | bytes 1574400 | tf_op jit(solution)/shard_map/dot_general | solution.py:70
  49.7 1.6 copy.35
  51.3 0.0 copy-start.5
  51.3 0.0 copy-start.6
  51.4 0.9 fusion.171
  52.3 0.6 fusion.170
  53.0 0.0 copy-done.5
  53.0 0.0 copy-done.6
  53.0 1.4 fusion.5
  54.4 0.0 copy-start.3
  54.4 0.3 reshape.29
  54.7 0.7 copy-done.3
  55.4 1.1 fusion.25
  56.5 0.1 reshape.31
  56.7 0.5 pad_maximum_fusion
  57.2 12.0 %copy.36 = f32[9,4,4,2048]{0,2,1,3:T(4,128)} copy(f32[9,4,4,2048]{3,2,1,0:T(4,128)S(1)} %pad_maximum_fusion) | data formatting | bytes 2359296 | tf_op jit(solution)/shard_map/concatenate | solution.py:127
  69.2 21.2 %reshape.33 = f32[16,1,18432]{2,1,0:T(1,128)} reshape(f32[2048,4,4,9]{3,2,1,0:T(4,128)} %bitcast.35) | data formatting | bytes 2359296
  90.5 6.1 %all-to-all-start.1 = ((f32[16,1,18432]{2,1,0:T(1,128)}), f32[16,1,18432]{2,1,0:T(1,128)S(1)}, u32[]{:S(2)}, u32[]{:S(2)}) async-start(f32[16,1,18432]{2,1,0:T(1,128)} %reshape.33), calls=%async_computation.1 | async-start | bytes 2359296 | tf_op jit(solution)/shard_map/all_to_all | solution.py:128
  96.6 1.9 collective-permute-start
  98.6 3.8 %collective-permute-start.1 = (f32[3,4,3,128]{3,2,1,0:T(4,128)S(1)}, f32[3,4,3,128]{3,2,1,0:T(4,128)S(1)}, u32[]{:S(2)}, u32[]{:S(2)}) collective-permute-start(f32[3,4,3,128]{3,2,1,0:T(4,128)S(1)} %get-tuple-element.19), channel_id=1, source_target_pairs={{1,0},{2,1},{3,2},{4,3},{5,4},{6,5},{7,6},{8,7},{9,8},{10,9},{11,1... | collective-permute-start | bytes 55304 | tf_op jit(solution)/shard_map/ppermute | solution.py:42
  102.4 1.3 collective-permute-done.1
  103.7 0.0 collective-permute-done
  103.8 0.1 broadcast_multiply_fusion
  103.9 0.1 pad_maximum_fusion.1
  103.9 1.4 fusion.1
  105.3 46.1 %all-to-all-done.1 = f32[16,1,18432]{2,1,0:T(1,128)S(1)} async-done(((f32[16,1,18432]{2,1,0:T(1,128)}), f32[16,1,18432]{2,1,0:T(1,128)S(1)}, u32[]{:S(2)}, u32[]{:S(2)}) %all-to-all-start.1) | async-done | bytes 1179680 | tf_op jit(solution)/shard_map/all_to_all | solution.py:128
  151.4 0.5 broadcast.202
  151.9 3.4 %reduce = f32[16,18432]{1,0:T(8,128)S(1)} reduce(f32[16,1,18432]{2,1,0:T(1,128)S(1)} %all-to-all-done.1, f32[]{:T(128)} %broadcast.202), dimensions={1}, to_apply=%all_to_all.25.reduce_sub_computation | reduce | bytes 2359300 | tf_op jit(solution)/shard_map/all_to_all | solution.py:128
  155.4 29.0 %reshape.34 = f32[2048,4,4,9]{3,2,1,0:T(4,128)} reshape(f32[16,18432]{1,0:T(8,128)S(1)} %reduce) | data formatting | bytes 2359296
  184.4 10.0 %copy.44 = f32[9,4,4,16,128]{4,3,2,1,0:T(8,128)S(1)} copy(f32[9,4,4,16,128]{0,2,1,4,3:T(4,128)} %bitcast.36) | data formatting | bytes 2359296 | tf_op jit(solution)/shard_map/all_to_all | solution.py:128
  194.4 0.1 fusion.169
  194.5 0.0 copy-start.4
  194.5 0.2 copy.38
  194.7 0.2 copy.39
  194.9 0.2 copy.40
  195.0 0.6 copy-done.1
  195.6 0.1 copy-done.4
  195.7 1.4 multiply_add_fusion
  (11 shorter events, 0.1 us)
Async XLA Ops:
  2.6 39.0 %all-to-all-start = ((f32[3,4,64,128]{3,1,0,2:T(4,128)}), f32[3,4,64,128]{3,1,0,2:T(4,128)S(1)}, u32[]{:S(2)}, u32[]{:S(2)}) async-start(f32[3,4,64,128]{3,1,0,2:T(4,128)} %copy.32), calls=%async_computation | async-start | bytes 786432 | tf_op jit(solution)/shard_map/all_to_all | solution.py:122
  44.6 1.4 copy-start.2
  51.3 1.6 copy-start.5
  51.3 1.6 copy-start.6
  54.4 1.0 copy-start.3
  90.5 6.1 %copy-start = (f32[3,4,64,128]{3,2,1,0:T(8,128)S(1)}, f32[3,4,64,128]{3,2,1,0:T(8,128)}, u32[]{:S(2)}) copy-start(f32[3,4,64,128]{3,2,1,0:T(8,128)} %param.2) | copy-start | bytes 1179652
  90.5 61.0 %all-to-all-start.1 = ((f32[16,1,18432]{2,1,0:T(1,128)}), f32[16,1,18432]{2,1,0:T(1,128)S(1)}, u32[]{:S(2)}, u32[]{:S(2)}) async-start(f32[16,1,18432]{2,1,0:T(1,128)} %reshape.33), calls=%async_computation.1 | async-start | bytes 2359296 | tf_op jit(solution)/shard_map/all_to_all | solution.py:128
  96.6 7.1 %collective-permute-start = (f32[3,4,3,128]{3,2,1,0:T(4,128)S(1)}, f32[3,4,3,128]{3,2,1,0:T(4,128)S(1)}, u32[]{:S(2)}, u32[]{:S(2)}) collective-permute-start(f32[3,4,3,128]{3,2,1,0:T(4,128)S(1)} %get-tuple-element.20), channel_id=1, source_target_pairs={{0,1},{1,2},{2,3},{3,4},{4,5},{5,6},{6,7},{7,8},{8,9},{9,10},{10,1... | collective-permute-start | bytes 55304 | tf_op jit(solution)/shard_map/ppermute | solution.py:40
  98.6 5.1 %collective-permute-start.1 = (f32[3,4,3,128]{3,2,1,0:T(4,128)S(1)}, f32[3,4,3,128]{3,2,1,0:T(4,128)S(1)}, u32[]{:S(2)}, u32[]{:S(2)}) collective-permute-start(f32[3,4,3,128]{3,2,1,0:T(4,128)S(1)} %get-tuple-element.19), channel_id=1, source_target_pairs={{1,0},{2,1},{3,2},{4,3},{5,4},{6,5},{7,6},{8,7},{9,8},{10,9},{11,1... | collective-permute-start | bytes 55304 | tf_op jit(solution)/shard_map/ppermute | solution.py:42
  194.5 1.1 copy-start.1
  194.5 1.2 copy-start.4
where the time goes:
time: 198 us; the launch traced here: 197 us
  local copies, waits for them, and re-layouts  82.7 us (42%)
  waiting for transfers between devices  71.1 us (36%)
  starting transfers between devices  27.1 us (14%)
  other arithmetic  9.69 us (5%)
  matrix products  5.65 us (3%)
    unnamed x18, local copies, waits for them, and re-layouts  55 us
    all_to_all x1, waiting for transfers between devices, local(): lax.all_to_all(result, 'gx', split_axis=3, concat_axis=2, tiled=True)  46.1 us
    all_to_all x1, waiting for transfers between devices, local(): lax.all_to_all(velocity, 'gx', split_axis=2, concat_axis=3, tiled=True)  23.8 us
    all_to_all x1, starting transfers between devices, local(): lax.all_to_all(velocity, 'gx', split_axis=2, concat_axis=3, tiled=True)  15.2 us
    concatenate x1, local copies, waits for them, and re-layouts, local(): result = jnp.concatenate([slope_part, curve_part], 0)  12 us
    all_to_all x2, local copies, waits for them, and re-layouts, local(): lax.all_to_all(result, 'gx', split_axis=3, concat_axis=2, tiled=True)  10.5 us
    all_to_all x1, starting transfers between devices, local(): lax.all_to_all(result, 'gx', split_axis=3, concat_axis=2, tiled=True)  6.13 us
    dot_general x2, matrix products, apply_matrix(): jnp.dot(flattened, matrix, precision=lax.Precision.HIGHEST, preferred_ele...  5.65 us
  transfers between devices with their start and end apart: 4, of which 3 were waited for; matrix products, arithmetic and copies ran while one was open for 1% of the time, Pallas kernels for 0%

commit v1 on v0

v1 whole, which is shorter than its diff:
```python
import math

import jax
import jax.numpy as jnp
import ml_dtypes
import numpy as np
from jax import lax
from jax.experimental import pallas as pl
from jax.experimental.pallas import tpu as pltpu
from jax.sharding import PartitionSpec as P

first_alpha = 1.0 / 3.0
first_near = 14.0 / 9.0
first_far = 1.0 / 9.0
second_alpha = 2.0 / 11.0
second_near = 12.0 / 11.0
second_far = 3.0 / 11.0
viscosity = 0.2
time_step = 0.25
gamma_now = 5.0 / 12.0
zeta_old = -17.0 / 60.0
first_stencil = (
    (1, 0.5 * first_near),
    (-1, -0.5 * first_near),
    (2, 0.25 * first_far),
    (-2, -0.25 * first_far),
)
second_stencil = (
    (0, -2.0 * second_near - 0.5 * second_far),
    (1, second_near),
    (-1, second_near),
    (2, 0.25 * second_far),
    (-2, 0.25 * second_far),
)
span_odd = (45.0 / 60.0, -9.0 / 60.0, 1.0 / 60.0)
span_even = (270.0 / 180.0, -27.0 / 180.0, 2.0 / 180.0)
span_centre = -490.0 / 180.0


def green(off_diag):
    root = (-1.0 + math.sqrt(1.0 - 4.0 * off_diag * off_diag)) / (2.0 * off_diag)
    return root, 1.0 / (1.0 + 2.0 * off_diag * root)


def weight_at(distance, stencil, off_diag):
    root, lead = green(off_diag)
    return sum(w * lead * root ** np.abs(distance + o) for o, w in stencil)


def reach_of(stencil, off_diag):
    root, lead = green(off_diag)
    return lead * sum(w * root**o for o, w in stencil)


def split_np(matrix):
    high = matrix.astype(ml_dtypes.bfloat16)
    low = (matrix - high.astype(np.float64)).astype(ml_dtypes.bfloat16)
    return high, low


def block_matrix(stencil, off_diag, extent):
    ids = np.arange(extent)
    return weight_at(ids[None, :] - ids[:, None], stencil, off_diag)


def inner_tables(extent):
    tables = []
    for stencil, off_diag in ((first_stencil, first_alpha), (second_stencil, second_alpha)):
        high, low = split_np(block_matrix(stencil, off_diag, extent))
        half = np.concatenate([high, low], 1)
        tables.append(np.concatenate([half, half], 0))
    return tables


def moment_table(extent):
    ids = np.arange(extent)
    rows = np.zeros((8, extent))
    for side, away in ((0, ids), (1, extent - 1 - ids)):
        rows[3 * side] = green(first_alpha)[0] ** away
        rows[3 * side + 1] = green(second_alpha)[0] ** away
        rows[3 * side + 2] = away == 0
    return rows.astype(np.float32)


def outer_table(extent):
    ids = np.arange(extent)
    table = np.zeros((16, 2 * extent))
    for side, away, sign in ((0, ids + 1, 1.0), (1, extent - ids, -1.0)):
        root1, root2 = green(first_alpha)[0], green(second_alpha)[0]
        far1 = reach_of(first_stencil, first_alpha) * root1**away
        far2 = reach_of(second_stencil, second_alpha) * root2**away
        near1 = (weight_at(np.array(1), first_stencil, first_alpha) - far1) * (away == 1)
        near2 = (weight_at(np.array(1), second_stencil, second_alpha) - far2) * (away == 1)
        row = 5 * side
        table[row, :extent] = sign * far1
        table[row + 1, extent:] = viscosity * far2
        table[row + 2, :extent] = sign * near1
        table[row + 2, extent:] = viscosity * near2
        table[row + 3, extent:] = -0.5 * sign * far1
        table[row + 4, extent:] = -0.5 * sign * near1
    high, low = split_np(table)
    return np.concatenate([high, high, low], 0)


def split(values):
    high = values.astype(jnp.bfloat16)
    low = (values - high.astype(jnp.float32)).astype(jnp.bfloat16)
    return high, low


def moments_kernel(vel_ref, table_ref, lower_ref, upper_ref):
    planes, rows, cols = vel_ref.shape[1:]
    lines = planes * rows
    nt = (((1,), (1,)), ((), ()))
    u = vel_ref[0].reshape(lines, cols)
    table = table_ref[...]
    for i in range(3):
        v = vel_ref[i].reshape(lines, cols)
        got = lax.dot_general(table, v, nt, precision=lax.Precision.HIGHEST, preferred_element_type=jnp.float32)
        flux = lax.dot_general(table, u * v, nt, precision=lax.Precision.HIGHEST, preferred_element_type=jnp.float32)
        at = slice(i * lines, (i + 1) * lines)
        lower_ref[0:3, at] = got[0:3]
        lower_ref[3:4, at] = flux[0:1]
        upper_ref[0:3, at] = got[3:6]
        upper_ref[3:4, at] = flux[3:4]


def mul_split(values, table):
    high, low = split(values)
    got = jnp.dot(jnp.concatenate([high, low], 1), table, preferred_element_type=jnp.float32)
    half = table.shape[1] // 2
    return got[:, :half] + got[:, half:]


def shifted(values, offset):
    planes, rows, cols = values.shape
    zeros = jnp.zeros((planes, abs(offset), cols), values.dtype)
    if offset > 0:
        return jnp.concatenate([values[:, offset:], zeros], 1)
    return jnp.concatenate([zeros, values[:, :offset]], 1)


def span_tap(v_far, w_near, w_far, distance, sign):
    odd = -0.5 * sign * span_odd[distance - 1]
    even = viscosity * span_even[distance - 1]
    return v_far * (odd * (w_near + w_far) + even)


def inner_kernel(vel_ref, first_ref, second_ref, part_ref):
    planes, rows, cols = vel_ref.shape[1:]
    lines = planes * rows
    u = vel_ref[0].reshape(lines, cols)
    w = vel_ref[2]
    for i in range(3):
        v3 = vel_ref[i]
        v = v3.reshape(lines, cols)
        slope = mul_split(v, first_ref[...])
        curve = mul_split(v, second_ref[...])
        flux = mul_split(u * v, first_ref[...])
        total = -0.5 * (u * slope + flux) + viscosity * curve
        total = total.reshape(planes, rows, cols) + (viscosity * span_centre) * v3
        for distance in (1, 2, 3):
            for sign in (1, -1):
                offset = sign * distance
                total = total + span_tap(shifted(v3, offset), w, shifted(w, offset), distance, sign)
        part_ref[i] = total


def outer_kernel(vel_ref, old_ref, part_ref, left_ref, right_ref, below_ref, above_ref, table_ref, new_ref, rhs_ref):
    planes, rows, cols = vel_ref.shape[1:]
    lines = planes * rows
    u = vel_ref[0].reshape(lines, cols)
    w = vel_ref[2]
    u_edge = (left_ref[2:3, :lines], right_ref[2:3, :lines])
    tn = (((0,), (0,)), ((), ()))
    for i in range(3):
        at = slice(i * lines, (i + 1) * lines)
        pieces = []
        for side, ref in ((0, left_ref), (1, right_ref)):
            got = ref[:, at]
            pieces += [got, got[2:3] * u_edge[side]]
        pieces.append(jnp.zeros((6, lines), jnp.float32))
        high, low = split(jnp.concatenate(pieces, 0))
        spread = lax.dot_general(
            jnp.concatenate([high, low, high], 0), table_ref[...], tn, preferred_element_type=jnp.float32
        )
        total = part_ref[i] + (spread[:, cols:] - 0.5 * u * spread[:, :cols]).reshape(planes, rows, cols)
        low_fix = jnp.zeros((planes, 8, cols), jnp.float32)
        high_fix = jnp.zeros((planes, 8, cols), jnp.float32)
        for d in (1, 2, 3):
            pad = jnp.zeros((planes, 8 - d, cols), jnp.float32)
            v_far = jnp.concatenate([below_ref[i, :, 3 - d :], pad], 1)
            w_far = jnp.concatenate([below_ref[2, :, 3 - d :], pad], 1)
            low_fix = low_fix + span_tap(v_far, w[:, :8], w_far, d, -1)
            v_far = jnp.concatenate([pad, above_ref[i, :, :d]], 1)
            w_far = jnp.concatenate([pad, above_ref[2, :, :d]], 1)
            high_fix = high_fix + span_tap(v_far, w[:, rows - 8 :], w_far, d, 1)
        total = jnp.concatenate(
            [total[:, :8] + low_fix, total[:, 8 : rows - 8], total[:, rows - 8 :] + high_fix], 1
        )
        rhs_ref[i] = total
        new_ref[i] = vel_ref[i] + (time_step * gamma_now) * total + (time_step * zeta_old) * old_ref[i]


def send(values, axis, step):
    count = lax.axis_size(axis)
    return lax.ppermute(values, axis, [(i, (i + step) % count) for i in range(count)])


def local(velocity, old_rhs):
    fields, planes, rows, cols = velocity.shape
    lines = planes * rows
    whole = pl.BlockSpec(memory_space=pltpu.VMEM)
    f32 = jnp.float32
    block = jax.ShapeDtypeStruct(velocity.shape, f32)
    side = jax.ShapeDtypeStruct((4, fields * lines), f32)
    params = pltpu.CompilerParams(vmem_limit_bytes=32 * 1024 * 1024)

    below = send(velocity[:, :, rows - 3 :], "gz", 1)
    above = send(velocity[:, :, :3], "gz", -1)
    lower, upper = pl.pallas_call(
        moments_kernel,
        out_shape=(side, side),
        in_specs=[whole] * 2,
        out_specs=(whole, whole),
        compiler_params=params,
        name="moments",
    )(velocity, jnp.asarray(moment_table(cols)))
    from_left = send(upper, "gx", 1)
    from_right = send(lower, "gx", -1)
    first, second = inner_tables(cols)
    part = pl.pallas_call(
        inner_kernel,
        out_shape=block,
        in_specs=[whole] * 3,
        out_specs=whole,
        compiler_params=params,
        cost_estimate=pl.CostEstimate(flops=600_000_000, bytes_accessed=1_000_000, transcendentals=0),
        name="inner",
    )(velocity, jnp.asarray(first), jnp.asarray(second))
    new_velocity, right_side = pl.pallas_call(
        outer_kernel,
        out_shape=(block, block),
        in_specs=[whole] * 8,
        out_specs=(whole, whole),
        compiler_params=params,
        name="outer",
    )(velocity, old_rhs, part, from_left, from_right, below, above, jnp.asarray(outer_table(cols)))
    return new_velocity, right_side


def solution(mesh):
    spec = P(None, None, "gz", "gx")
    return jax.shard_map(local, mesh=mesh, in_specs=(spec, spec), out_specs=(spec, spec), check_vma=False)
```

time: 198 us -> 29.3 us (0.15)
  the two profiles are of different devices: /device:TPU:6 before, /device:TPU:24 now
where the time goes in v1:
time: 29.3 us; the launch traced here: 29 us
  starting transfers between devices  19.4 us (66%)
  waiting for transfers between devices  4.43 us (15%)
  Pallas kernels  2.77 us (9%)
  local copies, waits for them, and re-layouts  1.71 us (6%)
  between operations  0.74 us (3%)
    ppermute x4, starting transfers between devices, send(): lax.ppermute(values, axis, [(i, (i + step) % count) for i in range(count)])  19.4 us
    ppermute x4, waiting for transfers between devices, send(): lax.ppermute(values, axis, [(i, (i + step) % count) for i in range(count)])  4.43 us
    unnamed x12, local copies, waits for them, and re-layouts  1.7 us
    pallas_call x1, Pallas kernels, local(): pl.pallas_call(outer_kernel, out_shape=(block, block), in_specs=[whole] *...  1.2 us
    pallas_call x1, Pallas kernels, local(): pl.pallas_call(inner_kernel, out_shape=block, in_specs=[whole] * 3, out_s...  0.84 us
    pallas_call x1, Pallas kernels, local(): pl.pallas_call(moments_kernel, out_shape=(side, side), in_specs=[whole] *...  0.73 us
  transfers between devices with their start and end apart: 4, of which 1 were waited for; matrix products, arithmetic and copies ran while one was open for 0% of the time, Pallas kernels for 3%

profile of v1, /device:TPU:24, one launch (start us, length us, event | category | flops | bytes accessed | tf_op | source)
XLA Modules:
  0.0 29.0 jit_solution(9980948884155864095)
XLA Ops:
  0.6 0.0 copy-start.3
  0.6 0.7 %copy-done.3 = f32[8,128]{1,0:T(8,128)S(1)} copy-done((f32[8,128]{1,0:T(8,128)S(1)}, f32[8,128]{1,0:T(8,128)}, u32[]{:S(2)}) %copy-start.3) | copy-done | bytes 4120
  1.3 0.0 copy-start
  1.3 1.0 %copy-done = f32[3,4,64,128]{3,2,1,0:T(8,128)S(1)} copy-done((f32[3,4,64,128]{3,2,1,0:T(8,128)S(1)}, f32[3,4,64,128]{3,2,1,0:T(8,128)}, u32[]{:S(2)}) %copy-start) | copy-done | bytes 393240
  2.3 0.0 copy-start.4
  2.3 0.0 copy-start.5
  2.3 0.7 %moments.1 = (f32[4,768]{1,0:T(4,128)S(1)}, f32[4,768]{1,0:T(4,128)S(1)}) custom-call(f32[3,4,64,128]{3,2,1,0:T(8,128)S(1)} %copy-done, f32[8,128]{1,0:T(8,128)S(1)} %copy-done.3), custom_call_target="tpu_custom_call" | custom-call | tf_op jit(solution)/shard_map/moments/pallas_call | solution.py:221
  3.0 3.8 %collective-permute-start = (f32[4,768]{1,0:T(4,128)S(1)}, f32[4,768]{1,0:T(4,128)S(1)}, u32[]{:S(2)}, u32[]{:S(2)}) collective-permute-start(f32[4,768]{1,0:T(4,128)S(1)} %get-tuple-element.4), channel_id=1, source_target_pairs={{0,32},{32,64},{64,96},{96,128},{128,160},{160,192},{192,224},{224... | collective-permute-start | bytes 36872 | tf_op jit(solution)/shard_map/ppermute | solution.py:207
  6.9 9.5 %collective-permute-start.1 = (f32[4,768]{1,0:T(4,128)S(1)}, f32[4,768]{1,0:T(4,128)S(1)}, u32[]{:S(2)}, u32[]{:S(2)}) collective-permute-start(f32[4,768]{1,0:T(4,128)S(1)} %get-tuple-element.5), channel_id=1, source_target_pairs={{0,480},{32,0},{64,32},{96,64},{128,96},{160,128},{192,160},{224,1... | collective-permute-start | bytes 36872 | tf_op jit(solution)/shard_map/ppermute | solution.py:207
  16.4 4.0 %collective-permute-start.3 = (f32[3,4,3,128]{3,2,1,0:T(4,128)S(1)}, f32[3,4,3,128]{3,2,1,0:T(4,128)S(1)}, u32[]{:S(2)}, u32[]{:S(2)}) collective-permute-start(f32[3,4,3,128]{3,2,1,0:T(4,128)S(1)} %get-tuple-element.6), channel_id=1, source_target_pairs={{0,31},{1,0},{2,1},{3,2},{4,3},{5,4},{6,5},{7,6},{8,7},{9,8},{10,9... | collective-permute-start | bytes 55304 | tf_op jit(solution)/shard_map/ppermute | solution.py:207
  20.4 0.0 copy-start.1
  20.4 0.0 copy-start.2
  20.4 2.1 %collective-permute-start.2 = (f32[3,4,3,128]{3,2,1,0:T(4,128)S(1)}, f32[3,4,3,128]{3,2,1,0:T(4,128)S(1)}, u32[]{:S(2)}, u32[]{:S(2)}) collective-permute-start(f32[3,4,3,128]{3,2,1,0:T(4,128)S(1)} %get-tuple-element.7), channel_id=1, source_target_pairs={{0,1},{1,2},{2,3},{3,4},{4,5},{5,6},{6,7},{7,8},{8,9},{9,10},{10,1... | collective-permute-start | bytes 55304 | tf_op jit(solution)/shard_map/ppermute | solution.py:207
  22.5 0.0 copy-done.4
  22.5 0.0 copy-done.5
  22.5 0.8 %inner.1.part_ref = f32[3,4,64,128]{3,2,1,0:T(8,128)S(1)} custom-call(f32[3,4,64,128]{3,2,1,0:T(8,128)S(1)} %copy-done, bf16[256,256]{1,0:T(8,128)(2,1)S(1)} %copy-done.5, bf16[256,256]{1,0:T(8,128)(2,1)S(1)} %copy-done.4), custom_call_target="tpu_custom_call" | custom-call | flops 600000000 | bytes 1000000 | tf_op jit(solution)/shard_map/inner/pallas_call | solution.py:232
  23.4 0.0 collective-permute-done.left_ref
  23.4 0.0 collective-permute-done.1.right_ref
  23.4 0.0 collective-permute-done.3.above_ref
  23.4 4.4 %collective-permute-done.2.below_ref = f32[3,4,3,128]{3,2,1,0:T(4,128)S(1)} collective-permute-done((f32[3,4,3,128]{3,2,1,0:T(4,128)S(1)}, f32[3,4,3,128]{3,2,1,0:T(4,128)S(1)}, u32[]{:S(2)}, u32[]{:S(2)}) %collective-permute-start.2) | collective-permute-done | bytes 18464 | tf_op jit(solution)/shard_map/ppermute | solution.py:207
  27.8 0.0 copy-done.1
  27.8 0.0 copy-done.2
  27.8 1.2 %outer.1 = (f32[3,4,64,128]{3,2,1,0:T(8,128)}, f32[3,4,64,128]{3,2,1,0:T(8,128)}) custom-call(f32[3,4,64,128]{3,2,1,0:T(8,128)S(1)} %copy-done, f32[3,4,64,128]{3,2,1,0:T(8,128)S(1)} %copy-done.1, f32[3,4,64,128]{3,2,1,0:T(8,128)S(1)} %inner.1.part_ref, f32[4,768]{1,0:T(4,128)S(1)} %collective-permute-done.left_ref, ...), custom_call_target="tpu_custom_call" | custom-call | tf_op jit(solution)/shard_map/outer/pallas_call | solution.py:241
  (1 shorter events, 0.0 us)
Async XLA Ops:
  0.6 0.7 %copy-start.3 = (f32[8,128]{1,0:T(8,128)S(1)}, f32[8,128]{1,0:T(8,128)}, u32[]{:S(2)}) copy-start(f32[8,128]{1,0:T(8,128)} %constant.8.clone.table_ref) | copy-start | bytes 12292
  1.3 1.0 %copy-start = (f32[3,4,64,128]{3,2,1,0:T(8,128)S(1)}, f32[3,4,64,128]{3,2,1,0:T(8,128)}, u32[]{:S(2)}) copy-start(f32[3,4,64,128]{3,2,1,0:T(8,128)} %vel_ref.5) | copy-start | bytes 1179652
  2.3 20.2 %copy-start.4 = (bf16[256,256]{1,0:T(8,128)(2,1)S(1)}, bf16[256,256]{1,0:T(8,128)(2,1)}, u32[]{:S(2)}) copy-start(bf16[256,256]{1,0:T(8,128)(2,1)} %constant.10.clone.second_ref) | copy-start | bytes 393220
  2.3 20.2 %copy-start.5 = (bf16[256,256]{1,0:T(8,128)(2,1)S(1)}, bf16[256,256]{1,0:T(8,128)(2,1)}, u32[]{:S(2)}) copy-start(bf16[256,256]{1,0:T(8,128)(2,1)} %constant.9.clone.first_ref) | copy-start | bytes 393220
  3.0 20.3 %collective-permute-start = (f32[4,768]{1,0:T(4,128)S(1)}, f32[4,768]{1,0:T(4,128)S(1)}, u32[]{:S(2)}, u32[]{:S(2)}) collective-permute-start(f32[4,768]{1,0:T(4,128)S(1)} %get-tuple-element.4), channel_id=1, source_target_pairs={{0,32},{32,64},{64,96},{96,128},{128,160},{160,192},{192,224},{224... | collective-permute-start | bytes 36872 | tf_op jit(solution)/shard_map/ppermute | solution.py:207
  6.9 16.5 %collective-permute-start.1 = (f32[4,768]{1,0:T(4,128)S(1)}, f32[4,768]{1,0:T(4,128)S(1)}, u32[]{:S(2)}, u32[]{:S(2)}) collective-permute-start(f32[4,768]{1,0:T(4,128)S(1)} %get-tuple-element.5), channel_id=1, source_target_pairs={{0,480},{32,0},{64,32},{96,64},{128,96},{160,128},{192,160},{224,1... | collective-permute-start | bytes 36872 | tf_op jit(solution)/shard_map/ppermute | solution.py:207
  16.4 7.0 %collective-permute-start.3 = (f32[3,4,3,128]{3,2,1,0:T(4,128)S(1)}, f32[3,4,3,128]{3,2,1,0:T(4,128)S(1)}, u32[]{:S(2)}, u32[]{:S(2)}) collective-permute-start(f32[3,4,3,128]{3,2,1,0:T(4,128)S(1)} %get-tuple-element.6), channel_id=1, source_target_pairs={{0,31},{1,0},{2,1},{3,2},{4,3},{5,4},{6,5},{7,6},{8,7},{9,8},{10,9... | collective-permute-start | bytes 55304 | tf_op jit(solution)/shard_map/ppermute | solution.py:207
  20.4 7.4 %copy-start.1 = (f32[3,4,64,128]{3,2,1,0:T(8,128)S(1)}, f32[3,4,64,128]{3,2,1,0:T(8,128)}, u32[]{:S(2)}) copy-start(f32[3,4,64,128]{3,2,1,0:T(8,128)} %old_ref.1) | copy-start | bytes 1179652
  20.4 7.4 %copy-start.2 = (bf16[48,256]{1,0:T(8,128)(2,1)S(1)}, bf16[48,256]{1,0:T(8,128)(2,1)}, u32[]{:S(2)}) copy-start(bf16[48,256]{1,0:T(8,128)(2,1)} %constant.11.clone.table_ref) | copy-start | bytes 73732
  20.4 7.4 %collective-permute-start.2 = (f32[3,4,3,128]{3,2,1,0:T(4,128)S(1)}, f32[3,4,3,128]{3,2,1,0:T(4,128)S(1)}, u32[]{:S(2)}, u32[]{:S(2)}) collective-permute-start(f32[3,4,3,128]{3,2,1,0:T(4,128)S(1)} %get-tuple-element.7), channel_id=1, source_target_pairs={{0,1},{1,2},{2,3},{3,4},{4,5},{5,6},{6,7},{7,8},{8,9},{9,10},{10,1... | collective-permute-start | bytes 55304 | tf_op jit(solution)/shard_map/ppermute | solution.py:207

commit v2 on v1

v2 whole, which is shorter than its diff:
```python
import functools
import math

import jax
import jax.numpy as jnp
from jax import lax
from jax.experimental import pallas as pl
from jax.experimental.pallas import tpu as pltpu
from jax.sharding import PartitionSpec as P

first_alpha = 1.0 / 3.0
first_near = 14.0 / 9.0
first_far = 1.0 / 9.0
second_alpha = 2.0 / 11.0
second_near = 12.0 / 11.0
second_far = 3.0 / 11.0
viscosity = 0.2
time_step = 0.25
gamma_now = 5.0 / 12.0
zeta_old = -17.0 / 60.0
first_stencil = (
    (1, 0.5 * first_near),
    (-1, -0.5 * first_near),
    (2, 0.25 * first_far),
    (-2, -0.25 * first_far),
)
second_stencil = (
    (0, -2.0 * second_near - 0.5 * second_far),
    (1, second_near),
    (-1, second_near),
    (2, 0.25 * second_far),
    (-2, 0.25 * second_far),
)
span_odd = (45.0 / 60.0, -9.0 / 60.0, 1.0 / 60.0)
span_even = (270.0 / 180.0, -27.0 / 180.0, 2.0 / 180.0)
span_centre = -490.0 / 180.0


def green(off_diag):
    root = (-1.0 + math.sqrt(1.0 - 4.0 * off_diag * off_diag)) / (2.0 * off_diag)
    return root, 1.0 / (1.0 + 2.0 * off_diag * root)


def weight_at(distance, stencil, off_diag):
    root, lead = green(off_diag)
    return sum(w * lead * root ** abs(distance + o) for o, w in stencil)


def reach_of(stencil, off_diag):
    root, lead = green(off_diag)
    return lead * sum(w * root**o for o, w in stencil)


def decay(away, off_diag):
    power = jnp.exp(away.astype(jnp.float32) * math.log(-green(off_diag)[0]))
    return jnp.where((away & 1) == 1, -power, power)


def block_matrix(stencil, off_diag, extent, odd):
    row = lax.broadcasted_iota(jnp.int32, (extent, extent), 0)
    column = lax.broadcasted_iota(jnp.int32, (extent, extent), 1)
    away = jnp.abs(column - row)
    far = reach_of(stencil, off_diag) * decay(away, off_diag)
    weight = jnp.where(away == 0, weight_at(0, stencil, off_diag), jnp.where(away == 1, weight_at(1, stencil, off_diag), far))
    if odd:
        weight = jnp.where(column < row, -weight, weight)
    half = jnp.concatenate(split(weight), 1)
    return jnp.concatenate([half, half], 0)


def outer_table(extent):
    row = lax.broadcasted_iota(jnp.int32, (16, 2 * extent), 0)
    column = lax.broadcasted_iota(jnp.int32, (16, 2 * extent), 1)
    left = row < 5
    kind = jnp.where(left, row, row - 5)
    slope = column < extent
    cell = jnp.where(slope, column, column - extent)
    away = jnp.where(left, cell + 1, extent - cell)
    sign = jnp.where(left, 1.0, -1.0)
    reach1, reach2 = reach_of(first_stencil, first_alpha), reach_of(second_stencil, second_alpha)
    near1 = weight_at(1, first_stencil, first_alpha) - reach1 * green(first_alpha)[0]
    near2 = weight_at(1, second_stencil, second_alpha) - reach2 * green(second_alpha)[0]
    touch = (away == 1).astype(jnp.float32)
    far1 = sign * reach1 * decay(away, first_alpha)
    far2 = viscosity * reach2 * decay(away, second_alpha)
    slopes = jnp.where(kind == 0, far1, jnp.where(kind == 2, sign * near1 * touch, 0.0))
    rests = jnp.where(kind == 1, far2, jnp.where(kind == 2, viscosity * near2 * touch, 0.0))
    rests = jnp.where(kind == 3, -0.5 * far1, jnp.where(kind == 4, -0.5 * sign * near1 * touch, rests))
    high, low = split(jnp.where(slope, slopes, rests))
    return jnp.concatenate([high, high, low], 0)


def split(values):
    high = values.astype(jnp.bfloat16)
    low = (values - high.astype(jnp.float32)).astype(jnp.bfloat16)
    return high, low


def moments_kernel(vel_ref, held_ref, lower_ref, upper_ref, outward_ref, inward_ref, sems):
    fields, planes, rows, cols = vel_ref.shape
    lines = planes * rows
    copies = [pltpu.make_async_copy(vel_ref.at[i], held_ref.at[i], sems.at[i]) for i in range(fields)]
    for copy in copies:
        copy.start()
    row = lax.broadcasted_iota(jnp.int32, (8, cols), 0)
    cell = lax.broadcasted_iota(jnp.int32, (8, cols), 1)
    away = jnp.where(row < 3, cell, cols - 1 - cell)
    kind = jnp.where(row < 3, row, row - 3)
    power = jnp.where(kind == 0, decay(away, first_alpha), decay(away, second_alpha))
    table = jnp.where(kind == 2, (away == 0).astype(jnp.float32), jnp.where(kind > 2, 0.0, power))
    high, low = split(table)
    both = jnp.concatenate([high, low], 0)
    odd = lax.rem(lax.axis_index("gz"), 2)
    nt = (((1,), (1,)), ((), ()))

    def moments(values):
        first, second = split(values)
        got = lax.dot_general(both, first, nt, preferred_element_type=jnp.float32)
        rest = lax.dot_general(both, second, nt, preferred_element_type=jnp.float32)
        return got[:8] + got[8:] + rest[:8]

    for i in range(fields):
        copies[i].wait()
        u = held_ref[0].reshape(lines, cols)
        v = held_ref[i].reshape(lines, cols)
        got = moments(v)
        flux = moments(u * v)
        at = slice(i * lines, (i + 1) * lines)
        lower_ref[0:3, at] = got[0:3]
        lower_ref[3:4, at] = flux[0:1]
        upper_ref[0:3, at] = got[3:6]
        upper_ref[3:4, at] = flux[3:4]
        head, tail = held_ref[i, :, :3], held_ref[i, :, rows - 3 :]
        inward_ref[i] = jnp.where(odd == 0, tail, head)
        outward_ref[i] = jnp.where(odd == 0, head, tail)


def mul_split(values, table):
    high, low = split(values)
    got = jnp.dot(jnp.concatenate([high, low], 1), table, preferred_element_type=jnp.float32)
    half = table.shape[1] // 2
    return got[:, :half] + got[:, half:]


def shifted(values, offset):
    planes, rows, cols = values.shape
    zeros = jnp.zeros((planes, abs(offset), cols), values.dtype)
    if offset > 0:
        return jnp.concatenate([values[:, offset:], zeros], 1)
    return jnp.concatenate([zeros, values[:, :offset]], 1)


def span_tap(v_far, w_near, w_far, distance, sign):
    odd = -0.5 * sign * span_odd[distance - 1]
    even = viscosity * span_even[distance - 1]
    return v_far * (odd * (w_near + w_far) + even)


def inner_kernel(vel_ref, old_ref, part_ref, base_ref, kept_ref, sem):
    copy = pltpu.make_async_copy(old_ref, kept_ref, sem)
    copy.start()
    planes, rows, cols = vel_ref.shape[1:]
    lines = planes * rows
    u = vel_ref[0].reshape(lines, cols)
    w = vel_ref[2]
    first = block_matrix(first_stencil, first_alpha, cols, True)
    second = block_matrix(second_stencil, second_alpha, cols, False)
    for i in range(3):
        v3 = vel_ref[i]
        v = v3.reshape(lines, cols)
        slope = mul_split(v, first)
        curve = mul_split(v, second)
        flux = mul_split(u * v, first)
        total = -0.5 * (u * slope + flux) + viscosity * curve
        total = total.reshape(planes, rows, cols) + (viscosity * span_centre) * v3
        for distance in (1, 2, 3):
            for sign in (1, -1):
                offset = sign * distance
                total = total + span_tap(shifted(v3, offset), w, shifted(w, offset), distance, sign)
        part_ref[i] = total
    copy.wait()
    for i in range(3):
        fresh = (time_step * gamma_now) * part_ref[i] + (time_step * zeta_old) * kept_ref[i]
        base_ref[i] = vel_ref[i] + fresh


def outer_kernel(
    vel_ref, left_ref, right_ref, early_out, early_in, early_part, early_base,
    late_out, late_in, late_part, late_base, new_ref, rhs_ref, new_held, rhs_held, halos, below_ref, above_ref, sems
):
    fields, planes, rows, cols = vel_ref.shape
    lines = planes * rows
    outs, ins = early_swaps(lax.axis_index("gx"))
    odd = lax.rem(lax.axis_index("gz"), 2) == 1

    def fetch(source, slot):
        return pltpu.make_async_copy(source, halos.at[slot], sems.at[slot])

    pl.when(outs)(lambda: fetch(early_out, 0).start())
    pl.when(jnp.logical_not(outs))(lambda: fetch(late_out, 0).start())
    pl.when(ins)(lambda: fetch(early_in, 1).start())
    pl.when(jnp.logical_not(ins))(lambda: fetch(late_in, 1).start())
    below_ref[...] = jnp.zeros(below_ref.shape, jnp.float32)
    above_ref[...] = jnp.zeros(above_ref.shape, jnp.float32)

    def across(part_ref, base_ref):
        u = vel_ref[0].reshape(lines, cols)
        u_edge = (left_ref[2:3, :lines], right_ref[2:3, :lines])
        table = outer_table(cols)
        tn = (((0,), (0,)), ((), ()))
        for i in range(fields):
            at = slice(i * lines, (i + 1) * lines)
            pieces = []
            for side, ref in ((0, left_ref), (1, right_ref)):
                got = ref[:, at]
                pieces += [got, got[2:3] * u_edge[side]]
            pieces.append(jnp.zeros((6, lines), jnp.float32))
            high, low = split(jnp.concatenate(pieces, 0))
            spread = lax.dot_general(
                jnp.concatenate([high, low, high], 0), table, tn, preferred_element_type=jnp.float32
            )
            extra = (spread[:, cols:] - 0.5 * u * spread[:, :cols]).reshape(planes, rows, cols)
            rhs_held[i] = part_ref[i] + extra
            new_held[i] = base_ref[i] + (time_step * gamma_now) * extra

    inner_early = jnp.logical_or(outs, ins)
    pl.when(inner_early)(lambda: across(early_part, early_base))
    pl.when(jnp.logical_not(inner_early))(lambda: across(late_part, late_base))
    fetch(early_out, 0).wait()
    fetch(early_in, 1).wait()
    below_ref[:, :, 0:3] = jnp.where(odd, halos[1], halos[0])
    above_ref[:, :, 8:11] = jnp.where(odd, halos[0], halos[1])
    w_low, w_high = vel_ref[2, :, 0:8], vel_ref[2, :, rows - 8 :]
    copies = []
    for i in range(fields):
        low_fix, high_fix = 0.0, 0.0
        for d in (1, 2, 3):
            near = slice(3 - d, 11 - d)
            low_fix = low_fix + span_tap(below_ref[i, :, near], w_low, below_ref[2, :, near], d, -1)
            near = slice(d, d + 8)
            high_fix = high_fix + span_tap(above_ref[i, :, near], w_high, above_ref[2, :, near], d, 1)
        for at, fix in ((slice(0, 8), low_fix), (slice(rows - 8, rows), high_fix)):
            rhs_held[i, :, at] += fix
            new_held[i, :, at] += (time_step * gamma_now) * fix
        for k, (source, target) in enumerate(((rhs_held, rhs_ref), (new_held, new_ref))):
            copies.append(pltpu.make_async_copy(source.at[i], target.at[i], sems.at[2 + 2 * i + k]))
            copies[-1].start()
    for copy in copies:
        copy.wait()


def send(values, axis, step):
    count = lax.axis_size(axis)
    return lax.ppermute(values, axis, [(i, (i + step) % count) for i in range(count)])


def swap(values, first, blocks):
    count = lax.axis_size("gz")
    pairs = []
    for x in blocks:
        for i in range(count // 2):
            a, b = (x * count + (2 * i + k + first) % count for k in (0, 1))
            pairs += [(a, b), (b, a)]
    return lax.ppermute(values, ("gx", "gz"), pairs)


def early_swaps(gx):
    return gx <= 1, (gx == 0) | (gx == 2)


def local(velocity, old_rhs):
    fields, planes, rows, cols = velocity.shape
    lines = planes * rows
    anywhere = pl.BlockSpec(memory_space=pl.ANY)
    whole = pl.BlockSpec(memory_space=pltpu.VMEM)
    f32 = jnp.float32
    block = pltpu.VMEM(velocity.shape, f32)
    side = pltpu.VMEM((4, fields * lines), f32)
    halo = pltpu.VMEM((fields, planes, 3, cols), f32)
    result = jax.ShapeDtypeStruct(velocity.shape, f32)
    params = pltpu.CompilerParams(vmem_limit_bytes=32 * 1024 * 1024)

    held, lower, upper, outward, inward = pl.pallas_call(
        moments_kernel,
        out_shape=(block, side, side, halo, halo),
        in_specs=[pl.BlockSpec(memory_space=pltpu.HBM)],
        out_specs=(whole,) * 5,
        scratch_shapes=[pltpu.SemaphoreType.DMA((fields,))],
        compiler_params=params,
        name="moments",
    )(pltpu.with_memory_space_constraint(velocity, pltpu.HBM))

    def inner(held, old):
        return pl.pallas_call(
            inner_kernel,
            out_shape=(block, block),
            in_specs=[whole, pl.BlockSpec(memory_space=pltpu.HBM)],
            out_specs=(whole, whole),
            scratch_shapes=[pltpu.VMEM(velocity.shape, f32), pltpu.SemaphoreType.DMA],
            compiler_params=params,
            cost_estimate=pl.CostEstimate(flops=600_000_000, bytes_accessed=1_000_000, transcendentals=0),
            name="inner",
        )(pltpu.with_memory_space_constraint(held, pltpu.VMEM), pltpu.with_memory_space_constraint(old, pltpu.HBM))

    def unset(*shapes):
        return pl.pallas_call(
            lambda *refs: None, out_shape=shapes, out_specs=(anywhere,) * len(shapes),
            compiler_params=params, name="unset",
        )()

    def after(arrays, *others):
        taken = [pltpu.with_memory_space_constraint(x, pltpu.VMEM) for x in (*arrays, *others)]
        return pl.pallas_call(
            lambda *refs: None,
            out_shape=tuple(pltpu.VMEM(x.shape, x.dtype) for x in arrays),
            in_specs=[anywhere] * len(taken),
            out_specs=(anywhere,) * len(arrays),
            input_output_aliases={i: i for i in range(len(arrays))},
            name="after",
        )(*taken)

    count = lax.axis_size("gx")
    outs, ins = early_swaps(lax.axis_index("gx"))
    kind = outs.astype(jnp.int32) + 2 * ins.astype(jnp.int32)
    chosen = [early_swaps(x) for x in range(count)]
    early_outs = [x for x in range(count) if chosen[x][0]]
    early_ins = [x for x in range(count) if chosen[x][1]]
    late_outs = [x for x in range(count) if not chosen[x][0]]
    late_ins = [x for x in range(count) if not chosen[x][1]]

    def stage(trades_out, trades_in, out_blocks, in_blocks, solves):
        def run(out, into, held, old):
            got = [swap(out, 1, out_blocks) if trades_out else None, swap(into, 0, in_blocks) if trades_in else None]
            blank = [halo] * (not trades_out) + [halo] * (not trades_in) + [block, block] * (not solves)
            solved = list(inner(held, old)) if solves else []
            blanks = list(unset(*blank)) if blank else []
            halves = [x if x is not None else blanks.pop(0) for x in got]
            return (*halves, *(solved or blanks))

        return run

    arrays = (outward, inward, held, old_rhs)
    early = lax.switch(
        kind, [stage(k in (1, 3), k in (2, 3), early_outs, early_ins, k > 0) for k in range(4)], *arrays
    )
    lower, upper = after((lower, upper), early[0], early[1])
    from_right = send(lower, "gx", -1)
    from_left = send(upper, "gx", 1)
    late = lax.switch(
        kind, [stage(k in (0, 2), k in (0, 1), late_outs, late_ins, k == 0) for k in range(4)], *arrays
    )
    scratch = pltpu.VMEM(velocity.shape, f32)
    inputs = [held, from_left, from_right, *early, *late]
    spaces = [pltpu.VMEM] * 3 + [pl.ANY, pl.ANY, pltpu.VMEM, pltpu.VMEM] * 2
    new_velocity, right_side = pl.pallas_call(
        outer_kernel,
        out_shape=(result, result),
        in_specs=[pl.BlockSpec(memory_space=x) for x in spaces],
        out_specs=(anywhere, anywhere),
        scratch_shapes=[
            scratch, scratch, pltpu.VMEM((2, *halo.shape), f32),
            *[pltpu.VMEM((fields, planes, 16, cols), f32)] * 2, pltpu.SemaphoreType.DMA((2 + 2 * fields,)),
        ],
        compiler_params=params,
        name="outer",
    )(*(pltpu.with_memory_space_constraint(x, y) for x, y in zip(inputs, spaces)))
    return new_velocity, right_side


def solution(mesh):
    spec = P(None, None, "gz", "gx")
    return jax.shard_map(local, mesh=mesh, in_specs=(spec, spec), out_specs=(spec, spec), check_vma=False)
```

time: 29.3 us -> 25.8 us (0.88)
  the two profiles are of different devices: /device:TPU:24 before, /device:TPU:33 now
where the time goes in v2:
time: 25.8 us; the launch traced here: 25.5 us
  starting transfers between devices  18.9 us (73%)
  Pallas kernels  4.5 us (17%)
  waiting for transfers between devices  1.34 us (5%)
  between operations  0.69 us (3%)
    ppermute x2, starting transfers between devices, send(): lax.ppermute(values, axis, [(i, (i + step) % count) for i in range(count)])  9.52 us
    ppermute x2, starting transfers between devices, swap(): return lax.ppermute(values, ('gx', 'gz'), pairs)  9.34 us
    pallas_call x1, Pallas kernels, local(): pl.pallas_call(outer_kernel, out_shape=(result, result), in_specs=[pl.Blo...  1.73 us
    pallas_call x1, Pallas kernels, local(): pl.pallas_call(moments_kernel, out_shape=(block, side, side, halo, halo),...  1.57 us
    ppermute x2, waiting for transfers between devices, swap(): return lax.ppermute(values, ('gx', 'gz'), pairs)  1.33 us
    pallas_call x1, Pallas kernels, inner(): pl.pallas_call(inner_kernel, out_shape=(block, block), in_specs=[whole, p...  1.2 us
  transfers between devices with their start and end apart: 4, of which 2 were waited for; matrix products, arithmetic and copies ran while one was open for 0% of the time, Pallas kernels for 5%

profile of v2, /device:TPU:33, one launch (start us, length us, event | category | flops | bytes accessed | tf_op | source)
XLA Modules:
  0.0 25.5 jit_solution(16945954942912208860)
XLA Ops:
  0.6 0.0 copy-start
  0.6 1.6 %moments.1 = (f32[3,4,64,128]{3,2,1,0:T(8,128)S(1)}, f32[4,768]{1,0:T(4,128)S(1)}, f32[4,768]{1,0:T(4,128)S(1)}, f32[3,4,3,128]{3,2,1,0:T(4,128)S(1)}, f32[3,4,3,128]{3,2,1,0:T(4,128)S(1)}) custom-call(f32[3,4,64,128]{3,2,1,0:T(8,128)} %vel_ref.1), custom_call_target="tpu_custom_call" | custom-call | tf_op jit(solution)/shard_map/moments/pallas_call | solution.py:283
  2.2 0.0 copy-done
  2.2 5.3 %conditional.2 = ((f32[3,4,3,128]{3,2,1,0:T(4,128)}, f32[3,4,3,128]{3,2,1,0:T(4,128)}, f32[3,4,64,128]{3,2,1,0:T(8,128)S(1)}, f32[3,4,64,128]{3,2,1,0:T(8,128)S(1)})) conditional(s32[]{:T(128)} %clamp.4, () %tuple.37, (f32[3,4,3,128]{3,2,1,0:T(4,128)S(1)}, f32[3,4,64,128]{3,2,1,0:T(8,128)S(1)}, ...), branch_computations={%region_0.0_spmd, %region_1.0_spmd, %region_2.0_spmd, %region_3.0_... | conditional | flops 600000000 | bytes 1147576 | solution.py:343
  2.3 3.7 %collective-permute-start = (f32[3,4,3,128]{3,2,1,0:T(4,128)S(1)}, f32[3,4,3,128]{3,2,1,0:T(4,128)}, u32[]{:S(2)}, u32[]{:S(2)}) collective-permute-start(f32[3,4,3,128]{3,2,1,0:T(4,128)S(1)} %get-tuple-element.30), channel_id=1, source_target_pairs={{1,2},{2,1},{3,4},{4,3},{5,6},{6,5},{7,8},{8,7},{9,10},{10,9},{11,... | collective-permute-start | bytes 55304 | tf_op jit(solution)/shard_map/cond/branch_1_fun/ppermute | solution.py:264
  6.0 1.2 %inner.4 = (f32[3,4,64,128]{3,2,1,0:T(8,128)S(1)}, f32[3,4,64,128]{3,2,1,0:T(8,128)S(1)}) custom-call(f32[3,4,64,128]{3,2,1,0:T(8,128)S(1)} %get-tuple-element.31.vel_ref, f32[3,4,64,128]{3,2,1,0:T(8,128)S(1)} %get-tuple-element.32.old_ref), custom_call_target="tpu_custom_call" | custom-call | flops 600000000 | bytes 1000000 | tf_op jit(solution)/shard_map/cond/branch_1_fun/inner/pallas_call | solution.py:294
  7.2 0.4 %collective-permute-done = f32[3,4,3,128]{3,2,1,0:T(4,128)} collective-permute-done((f32[3,4,3,128]{3,2,1,0:T(4,128)S(1)}, f32[3,4,3,128]{3,2,1,0:T(4,128)}, u32[]{:S(2)}, u32[]{:S(2)}) %collective-permute-start) | collective-permute-done | bytes 18464 | tf_op jit(solution)/shard_map/cond/branch_1_fun/ppermute | solution.py:264
  7.6 2.1 %collective-permute-start.8 = (f32[4,768]{1,0:T(4,128)S(1)}, f32[4,768]{1,0:T(4,128)S(1)}, u32[]{:S(2)}, u32[]{:S(2)}) collective-permute-start(f32[4,768]{1,0:T(4,128)S(1)} %get-tuple-element.82), channel_id=1, source_target_pairs={{0,32},{32,64},{64,96},{96,128},{128,160},{160,192},{192,224},{224... | collective-permute-start | bytes 36872 | tf_op jit(solution)/shard_map/ppermute | solution.py:254
  9.7 7.4 %collective-permute-start.9 = (f32[4,768]{1,0:T(4,128)S(1)}, f32[4,768]{1,0:T(4,128)S(1)}, u32[]{:S(2)}, u32[]{:S(2)}) collective-permute-start(f32[4,768]{1,0:T(4,128)S(1)} %get-tuple-element.83), channel_id=1, source_target_pairs={{0,480},{32,0},{64,32},{96,64},{128,96},{160,128},{192,160},{224,1... | collective-permute-start | bytes 36872 | tf_op jit(solution)/shard_map/ppermute | solution.py:254
  17.1 6.7 %conditional.3 = ((f32[3,4,3,128]{3,2,1,0:T(4,128)}, f32[3,4,3,128]{3,2,1,0:T(4,128)}, f32[3,4,64,128]{3,2,1,0:T(8,128)S(1)}, f32[3,4,64,128]{3,2,1,0:T(8,128)S(1)})) conditional(s32[]{:T(128)} %clamp.4, (f32[3,4,3,128]{3,2,1,0:T(4,128)S(1)}, f32[3,4,3,128]{3,2,1,0:T(4,128)S(1)}, f32[3,4,64,128]{3,2,1,0:T(8,128)S(1)}, ...), branch_computations={%region_4.0_spmd, %region_5.0_spmd, %region_6.0_spmd, %region_7.0_... | conditional | flops 600000000 | bytes 2720468 | solution.py:349
  17.1 5.7 %collective-permute-start.6 = (f32[3,4,3,128]{3,2,1,0:T(4,128)S(1)}, f32[3,4,3,128]{3,2,1,0:T(4,128)}, u32[]{:S(2)}, u32[]{:S(2)}) collective-permute-start(f32[3,4,3,128]{3,2,1,0:T(4,128)S(1)} %param.5), channel_id=1, source_target_pairs={{32,33},{33,32},{34,35},{35,34},{36,37},{37,36},{38,39},{39,38},{4... | collective-permute-start | bytes 55304 | tf_op jit(solution)/shard_map/cond/branch_1_fun/ppermute | solution.py:264
  22.8 0.9 %collective-permute-done.6 = f32[3,4,3,128]{3,2,1,0:T(4,128)} collective-permute-done((f32[3,4,3,128]{3,2,1,0:T(4,128)S(1)}, f32[3,4,3,128]{3,2,1,0:T(4,128)}, u32[]{:S(2)}, u32[]{:S(2)}) %collective-permute-start.6) | collective-permute-done | bytes 18464 | tf_op jit(solution)/shard_map/cond/branch_1_fun/ppermute | solution.py:264
  23.7 0.0 collective-permute-done.8.left_ref
  23.8 0.0 collective-permute-done.9.right_ref
  23.8 1.7 %outer.1 = (f32[3,4,64,128]{3,2,1,0:T(8,128)}, f32[3,4,64,128]{3,2,1,0:T(8,128)}) custom-call(f32[3,4,64,128]{3,2,1,0:T(8,128)S(1)} %get-tuple-element.75.vel_ref, f32[4,768]{1,0:T(4,128)S(1)} %collective-permute-done.8.left_ref, f32[4,768]{1,0:T(4,128)S(1)} %collective-permute-done.9.right_ref, f32[3,4,3,128]{3,2,1,0:T(4,128)} %get-tuple-element.80.refs_2_.early_out, ...), custom_call_target="tpu_custom_call" | custom-call | tf_op jit(solution)/shard_map/outer/pallas_call | solution.py:355
  (3 shorter events, 0.0 us)
Async XLA Ops:
  0.6 1.6 %copy-start = (f32[3,4,64,128]{3,2,1,0:T(8,128)S(1)}, f32[3,4,64,128]{3,2,1,0:T(8,128)}, u32[]{:S(2)}) copy-start(f32[3,4,64,128]{3,2,1,0:T(8,128)} %param.11) | copy-start | bytes 1179652
  2.3 5.3 %collective-permute-start = (f32[3,4,3,128]{3,2,1,0:T(4,128)S(1)}, f32[3,4,3,128]{3,2,1,0:T(4,128)}, u32[]{:S(2)}, u32[]{:S(2)}) collective-permute-start(f32[3,4,3,128]{3,2,1,0:T(4,128)S(1)} %get-tuple-element.30), channel_id=1, source_target_pairs={{1,2},{2,1},{3,4},{4,3},{5,6},{6,5},{7,8},{8,7},{9,10},{10,9},{11,... | collective-permute-start | bytes 55304 | tf_op jit(solution)/shard_map/cond/branch_1_fun/ppermute | solution.py:264
  7.6 16.2 %collective-permute-start.8 = (f32[4,768]{1,0:T(4,128)S(1)}, f32[4,768]{1,0:T(4,128)S(1)}, u32[]{:S(2)}, u32[]{:S(2)}) collective-permute-start(f32[4,768]{1,0:T(4,128)S(1)} %get-tuple-element.82), channel_id=1, source_target_pairs={{0,32},{32,64},{64,96},{96,128},{128,160},{160,192},{192,224},{224... | collective-permute-start | bytes 36872 | tf_op jit(solution)/shard_map/ppermute | solution.py:254
  9.7 14.1 %collective-permute-start.9 = (f32[4,768]{1,0:T(4,128)S(1)}, f32[4,768]{1,0:T(4,128)S(1)}, u32[]{:S(2)}, u32[]{:S(2)}) collective-permute-start(f32[4,768]{1,0:T(4,128)S(1)} %get-tuple-element.83), channel_id=1, source_target_pairs={{0,480},{32,0},{64,32},{96,64},{128,96},{160,128},{192,160},{224,1... | collective-permute-start | bytes 36872 | tf_op jit(solution)/shard_map/ppermute | solution.py:254
  17.1 6.6 %collective-permute-start.6 = (f32[3,4,3,128]{3,2,1,0:T(4,128)S(1)}, f32[3,4,3,128]{3,2,1,0:T(4,128)}, u32[]{:S(2)}, u32[]{:S(2)}) collective-permute-start(f32[3,4,3,128]{3,2,1,0:T(4,128)S(1)} %param.5), channel_id=1, source_target_pairs={{32,33},{33,32},{34,35},{35,34},{36,37},{37,36},{38,39},{39,38},{4... | collective-permute-start | bytes 55304 | tf_op jit(solution)/shard_map/cond/branch_1_fun/ppermute | solution.py:264

commit v3 on v2

--- a/solution.py
+++ b/solution.py
@@ -96,12 +96,16 @@
     return high, low
 
 
-def moments_kernel(vel_ref, held_ref, lower_ref, upper_ref, outward_ref, inward_ref, sems):
+def moments_kernel(vel_ref, held_ref, first_ref, second_ref, third_ref, outward_ref, inward_ref, sems):
     fields, planes, rows, cols = vel_ref.shape
     lines = planes * rows
-    copies = [pltpu.make_async_copy(vel_ref.at[i], held_ref.at[i], sems.at[i]) for i in range(fields)]
-    for copy in copies:
-        copy.start()
+    copies = [
+        [pltpu.make_async_copy(vel_ref.at[i, p], held_ref.at[i, p], sems.at[planes * i + p]) for p in range(planes)]
+        for i in range(fields)
+    ]
+    for i in range(fields):
+        for copy in copies[i]:
+            copy.start()
     row = lax.broadcasted_iota(jnp.int32, (8, cols), 0)
     cell = lax.broadcasted_iota(jnp.int32, (8, cols), 1)
     away = jnp.where(row < 3, cell, cols - 1 - cell)
@@ -110,7 +114,9 @@
     table = jnp.where(kind == 2, (away == 0).astype(jnp.float32), jnp.where(kind > 2, 0.0, power))
     high, low = split(table)
     both = jnp.concatenate([high, low], 0)
-    odd = lax.rem(lax.axis_index("gz"), 2)
+    gx, gz = lax.axis_index("gx"), lax.axis_index("gz")
+    odd = lax.rem(gz, 2)
+    first_up, second_up = upward_steps(gx, gz)
     nt = (((1,), (1,)), ((), ()))
 
     def moments(values):
@@ -120,16 +126,18 @@
         return got[:8] + got[8:] + rest[:8]
 
     for i in range(fields):
-        copies[i].wait()
+        for copy in copies[i]:
+            copy.wait()
         u = held_ref[0].reshape(lines, cols)
         v = held_ref[i].reshape(lines, cols)
         got = moments(v)
         flux = moments(u * v)
         at = slice(i * lines, (i + 1) * lines)
-        lower_ref[0:3, at] = got[0:3]
-        lower_ref[3:4, at] = flux[0:1]
-        upper_ref[0:3, at] = got[3:6]
-        upper_ref[3:4, at] = flux[3:4]
+        lower = jnp.concatenate([got[0:3], flux[0:1]], 0)
+        upper = jnp.concatenate([got[3:6], flux[3:4]], 0)
+        first_ref[:, at] = jnp.where(first_up, upper, lower)
+        second_ref[:, at] = jnp.where(second_up, upper, lower)
+        third_ref[:, at] = lower
         head, tail = held_ref[i, :, :3], held_ref[i, :, rows - 3 :]
         inward_ref[i] = jnp.where(odd == 0, tail, head)
         outward_ref[i] = jnp.where(odd == 0, head, tail)
@@ -185,54 +193,57 @@
 
 
 def outer_kernel(
-    vel_ref, left_ref, right_ref, early_out, early_in, early_part, early_base,
-    late_out, late_in, late_part, late_base, new_ref, rhs_ref, new_held, rhs_held, halos, below_ref, above_ref, sems
+    vel_ref, first_ref, second_ref, third_ref, part_ref, base_ref, early_out, early_in, late_out, late_in,
+    new_ref, rhs_ref, new_held, rhs_held, halos, below_ref, above_ref, sems
 ):
     fields, planes, rows, cols = vel_ref.shape
     lines = planes * rows
-    outs, ins = early_swaps(lax.axis_index("gx"))
+    lowest = lax.axis_index("gx") == 0
     odd = lax.rem(lax.axis_index("gz"), 2) == 1
 
     def fetch(source, slot):
         return pltpu.make_async_copy(source, halos.at[slot], sems.at[slot])
 
-    pl.when(outs)(lambda: fetch(early_out, 0).start())
-    pl.when(jnp.logical_not(outs))(lambda: fetch(late_out, 0).start())
-    pl.when(ins)(lambda: fetch(early_in, 1).start())
-    pl.when(jnp.logical_not(ins))(lambda: fetch(late_in, 1).start())
+    @pl.when(lowest)
+    def _():
+        fetch(early_out, 0).start()
+        fetch(early_in, 1).start()
+
+    @pl.when(jnp.logical_not(lowest))
+    def _():
+        fetch(late_out, 0).start()
+        fetch(late_in, 1).start()
+
     below_ref[...] = jnp.zeros(below_ref.shape, jnp.float32)
     above_ref[...] = jnp.zeros(above_ref.shape, jnp.float32)
-
-    def across(part_ref, base_ref):
-        u = vel_ref[0].reshape(lines, cols)
-        u_edge = (left_ref[2:3, :lines], right_ref[2:3, :lines])
-        table = outer_table(cols)
-        tn = (((0,), (0,)), ((), ()))
-        for i in range(fields):
-            at = slice(i * lines, (i + 1) * lines)
-            pieces = []
-            for side, ref in ((0, left_ref), (1, right_ref)):
-                got = ref[:, at]
-                pieces += [got, got[2:3] * u_edge[side]]
-            pieces.append(jnp.zeros((6, lines), jnp.float32))
-            high, low = split(jnp.concatenate(pieces, 0))
-            spread = lax.dot_general(
-                jnp.concatenate([high, low, high], 0), table, tn, preferred_element_type=jnp.float32
-            )
-            extra = (spread[:, cols:] - 0.5 * u * spread[:, :cols]).reshape(planes, rows, cols)
-            rhs_held[i] = part_ref[i] + extra
-            new_held[i] = base_ref[i] + (time_step * gamma_now) * extra
-
-    inner_early = jnp.logical_or(outs, ins)
-    pl.when(inner_early)(lambda: across(early_part, early_base))
-    pl.when(jnp.logical_not(inner_early))(lambda: across(late_part, late_base))
-    fetch(early_out, 0).wait()
-    fetch(early_in, 1).wait()
-    below_ref[:, :, 0:3] = jnp.where(odd, halos[1], halos[0])
-    above_ref[:, :, 8:11] = jnp.where(odd, halos[0], halos[1])
-    w_low, w_high = vel_ref[2, :, 0:8], vel_ref[2, :, rows - 8 :]
+    u = vel_ref[0].reshape(lines, cols)
+    gx, gz = lax.axis_index("gx"), lax.axis_index("gz")
+    even = lax.rem(gx, 2) == 0
+    first, second, third = first_ref[...], second_ref[...], third_ref[...]
+    left = jnp.where(jnp.where(gz == 0, even, gx == 1), first, second)
+    right = jnp.where(gx == lax.axis_size("gx") - 1, third, jnp.where(even, second, first))
+    right = jnp.where(gz == 0, right, jnp.where(gx == 0, first, third))
+    u_edge = (left[2:3, :lines], right[2:3, :lines])
+    table = outer_table(cols)
+    tn = (((0,), (0,)), ((), ()))
     copies = []
-    for i in range(fields):
+
+    def across(i):
+        at = slice(i * lines, (i + 1) * lines)
+        pieces = []
+        for side, got in ((0, left[:, at]), (1, right[:, at])):
+            pieces += [got, got[2:3] * u_edge[side]]
+        pieces.append(jnp.zeros((6, lines), jnp.float32))
+        high, low = split(jnp.concatenate(pieces, 0))
+        spread = lax.dot_general(
+            jnp.concatenate([high, low, high], 0), table, tn, preferred_element_type=jnp.float32
+        )
+        extra = (spread[:, cols:] - 0.5 * u * spread[:, :cols]).reshape(planes, rows, cols)
+        rhs_held[i] = part_ref[i] + extra
+        new_held[i] = base_ref[i] + (time_step * gamma_now) * extra
+
+    def along(i):
+        w_low, w_high = vel_ref[2, :, 0:8], vel_ref[2, :, rows - 8 :]
         low_fix, high_fix = 0.0, 0.0
         for d in (1, 2, 3):
             near = slice(3 - d, 11 - d)
@@ -245,13 +256,45 @@
         for k, (source, target) in enumerate(((rhs_held, rhs_ref), (new_held, new_ref))):
             copies.append(pltpu.make_async_copy(source.at[i], target.at[i], sems.at[2 + 2 * i + k]))
             copies[-1].start()
+
+    across(0)
+    across(1)
+    fetch(early_out, 0).wait()
+    fetch(early_in, 1).wait()
+    below_ref[:, :, 0:3] = jnp.where(odd, halos[1], halos[0])
+    above_ref[:, :, 8:11] = jnp.where(odd, halos[0], halos[1])
+    along(0)
+    along(1)
+    across(2)
+    along(2)
     for copy in copies:
         copy.wait()
 
 
-def send(values, axis, step):
-    count = lax.axis_size(axis)
-    return lax.ppermute(values, axis, [(i, (i + step) % count) for i in range(count)])
+def upward_steps(gx, gz):
+    even = lax.rem(gx, 2) == 0
+    first = jnp.where(gz == 0, jnp.logical_not(even), gx == 0)
+    return first, jnp.logical_or(gz > 0, even)
+
+
+def step_pairs(xs, zs):
+    up = lambda x, z: ((x, z), ((x + 1) % xs, z))
+    down = lambda x, z: ((x, z), ((x - 1) % xs, z))
+    first, second, third = [], [], []
+    for z in range(1, zs):
+        first += [up(0, z), down(1, z)]
+        second += [up(x, z) for x in range(1, xs)]
+        third += [down(x, z) for x in range(2, xs)] + [down(0, z)]
+    for x in range(0, xs, 2):
+        first += [up((x - 1) % xs, 0)] + [down(x, 0)] * (x > 0)
+        second += [up(x, 0), down(x + 1, 0)]
+    third += [down(0, 0)]
+    return first, second, third
+
+
+def permute(values, pairs):
+    count = lax.axis_size("gz")
+    return lax.ppermute(values, ("gx", "gz"), [(a * count + b, c * count + d) for (a, b), (c, d) in pairs])
 
 
 def swap(values, first, blocks):
@@ -259,13 +302,9 @@
     pairs = []
     for x in blocks:
         for i in range(count // 2):
-            a, b = (x * count + (2 * i + k + first) % count for k in (0, 1))
+            a, b = ((x, (2 * i + k + first) % count) for k in (0, 1))
             pairs += [(a, b), (b, a)]
-    return lax.ppermute(values, ("gx", "gz"), pairs)
-
-
-def early_swaps(gx):
-    return gx <= 1, (gx == 0) | (gx == 2)
+    return permute(values, pairs)
 
 
 def local(velocity, old_rhs):
@@ -280,12 +319,12 @@
     result = jax.ShapeDtypeStruct(velocity.shape, f32)
     params = pltpu.CompilerParams(vmem_limit_bytes=32 * 1024 * 1024)
 
-    held, lower, upper, outward, inward = pl.pallas_call(
+    held, first, second, third, outward, inward = pl.pallas_call(
         moments_kernel,
-        out_shape=(block, side, side, halo, halo),
+        out_shape=(block, side, side, side, halo, halo),
         in_specs=[pl.BlockSpec(memory_space=pltpu.HBM)],
-        out_specs=(whole,) * 5,
-        scratch_shapes=[pltpu.SemaphoreType.DMA((fields,))],
+        out_specs=(whole,) * 6,
+        scratch_shapes=[pltpu.SemaphoreType.DMA((fields * planes,))],
         compiler_params=params,
         name="moments",
     )(pltpu.with_memory_space_constraint(velocity, pltpu.HBM))
@@ -319,39 +358,33 @@
             name="after",
         )(*taken)
 
-    count = lax.axis_size("gx")
-    outs, ins = early_swaps(lax.axis_index("gx"))
-    kind = outs.astype(jnp.int32) + 2 * ins.astype(jnp.int32)
-    chosen = [early_swaps(x) for x in range(count)]
-    early_outs = [x for x in range(count) if chosen[x][0]]
-    early_ins = [x for x in range(count) if chosen[x][1]]
-    late_outs = [x for x in range(count) if not chosen[x][0]]
-    late_ins = [x for x in range(count) if not chosen[x][1]]
-
-    def stage(trades_out, trades_in, out_blocks, in_blocks, solves):
-        def run(out, into, held, old):
-            got = [swap(out, 1, out_blocks) if trades_out else None, swap(into, 0, in_blocks) if trades_in else None]
-            blank = [halo] * (not trades_out) + [halo] * (not trades_in) + [block, block] * (not solves)
-            solved = list(inner(held, old)) if solves else []
-            blanks = list(unset(*blank)) if blank else []
-            halves = [x if x is not None else blanks.pop(0) for x in got]
-            return (*halves, *(solved or blanks))
-
-        return run
-
-    arrays = (outward, inward, held, old_rhs)
-    early = lax.switch(
-        kind, [stage(k in (1, 3), k in (2, 3), early_outs, early_ins, k > 0) for k in range(4)], *arrays
-    )
-    lower, upper = after((lower, upper), early[0], early[1])
-    from_right = send(lower, "gx", -1)
-    from_left = send(upper, "gx", 1)
-    late = lax.switch(
-        kind, [stage(k in (0, 2), k in (0, 1), late_outs, late_ins, k == 0) for k in range(4)], *arrays
-    )
+    xs, zs = lax.axis_size("gx"), lax.axis_size("gz")
+    gx = lax.axis_index("gx")
+    steps = step_pairs(xs, zs)
+    rest = range(1, xs)
+
+    def early_swaps(out, into):
+        return after((swap(out, 1, [0]), swap(into, 0, [0])))
+
+    def early_none(out, into):
+        return unset(halo, halo)
+
+    def late_none(out, into, held, old):
+        return (*unset(halo, halo), *inner(held, old))
+
+    def late_swaps(out, into, held, old):
+        solved = inner(held, old)
+        return (*after((swap(out, 1, rest), swap(into, 0, rest))), *solved)
+
+    second = permute(second, steps[1])
+    first = permute(first, steps[0])
+    early = lax.cond(gx == 0, early_swaps, early_none, outward, inward)
+    (third,) = after((third,), *early)
+    third = permute(third, steps[2])
+    late_out, late_in, part, base = lax.cond(gx == 0, late_none, late_swaps, outward, inward, held, old_rhs)
     scratch = pltpu.VMEM(velocity.shape, f32)
-    inputs = [held, from_left, from_right, *early, *late]
-    spaces = [pltpu.VMEM] * 3 + [pl.ANY, pl.ANY, pltpu.VMEM, pltpu.VMEM] * 2
+    inputs = [held, first, second, third, part, base, *early, late_out, late_in]
+    spaces = [pltpu.VMEM] * 6 + [pl.ANY] * 4
     new_velocity, right_side = pl.pallas_call(
         outer_kernel,
         out_shape=(result, result),

time: 25.8 us -> 22.6 us (0.88)
  the two profiles are of different devices: /device:TPU:33 before, /device:TPU:1 now
where the time goes in v3:
time: 22.6 us; the launch traced here: 22.2 us
  starting transfers between devices  16.1 us (71%)
  Pallas kernels  4.41 us (20%)
  waiting for transfers between devices  0.96 us (4%)
  between operations  0.7 us (3%)
    ppermute x5, starting transfers between devices, permute(): lax.ppermute(values, ('gx', 'gz'), [(a * count + b, c * count + d) for (a...  16.1 us
    pallas_call x1, Pallas kernels, local(): pl.pallas_call(outer_kernel, out_shape=(result, result), in_specs=[pl.Blo...  1.81 us
    pallas_call x1, Pallas kernels, local(): pl.pallas_call(moments_kernel, out_shape=(block, side, side, side, halo,...  1.51 us
    pallas_call x1, Pallas kernels, inner(): pl.pallas_call(inner_kernel, out_shape=(block, block), in_specs=[whole, p...  1.09 us
    ppermute x5, waiting for transfers between devices, permute(): lax.ppermute(values, ('gx', 'gz'), [(a * count + b, c * count + d) for (a...  0.96 us
  transfers between devices with their start and end apart: 5, of which 1 were waited for; matrix products, arithmetic and copies ran while one was open for 0% of the time, Pallas kernels for 5%

profile of v3, /device:TPU:1, one launch (start us, length us, event | category | flops | bytes accessed | tf_op | source)
XLA Modules:
  0.0 22.2 jit_solution(5706344037842538795)
XLA Ops:
  0.6 1.5 %moments.1 = (f32[3,4,64,128]{3,2,1,0:T(8,128)S(1)}, f32[4,768]{1,0:T(4,128)S(1)}, f32[4,768]{1,0:T(4,128)S(1)}, f32[4,768]{1,0:T(4,128)S(1)}, f32[3,4,3,128]{3,...) custom-call(f32[3,4,64,128]{3,2,1,0:T(8,128)} %vel_ref.1), custom_call_target="tpu_custom_call" | custom-call | tf_op jit(solution)/shard_map/moments/pallas_call | solution.py:322
  2.1 4.4 %collective-permute-start.4 = (f32[4,768]{1,0:T(4,128)S(1)}, f32[4,768]{1,0:T(4,128)S(1)}, u32[]{:S(2)}, u32[]{:S(2)}) collective-permute-start(f32[4,768]{1,0:T(4,128)S(1)} %get-tuple-element.47), channel_id=1, source_target_pairs={{1,33},{33,1},{2,34},{34,2},{3,35},{35,3},{4,36},{36,4},{5,37},{37... | collective-permute-start | bytes 36872 | tf_op jit(solution)/shard_map/ppermute | solution.py:297
  6.5 1.3 %collective-permute-start.5 = (f32[4,768]{1,0:T(4,128)S(1)}, f32[4,768]{1,0:T(4,128)S(1)}, u32[]{:S(2)}, u32[]{:S(2)}) collective-permute-start(f32[4,768]{1,0:T(4,128)S(1)} %get-tuple-element.48), channel_id=1, source_target_pairs={{33,65},{65,97},{97,129},{129,161},{161,193},{193,225},{225,257},{... | collective-permute-start | bytes 36872 | tf_op jit(solution)/shard_map/ppermute | solution.py:297
  7.8 10.1 %conditional.2 = ((f32[3,4,3,128]{3,2,1,0:T(4,128)}, f32[3,4,3,128]{3,2,1,0:T(4,128)})) conditional(s32[]{:T(128)} %convert_element_type.4, () %tuple.21, (f32[3,4,3,128]{3,2,1,0:T(4,128)S(1)}, f32[3,4,3,128]{3,2,1,0:T(4,128)S(1)}) %tuple.22), branch_computations={%region_0.0_spmd, %region_1.0_spmd} | conditional | bytes 147544 | solution.py:381
  7.8 4.0 %collective-permute-start = (f32[3,4,3,128]{3,2,1,0:T(4,128)S(1)}, f32[3,4,3,128]{3,2,1,0:T(4,128)}, u32[]{:S(2)}, u32[]{:S(2)}) collective-permute-start(f32[3,4,3,128]{3,2,1,0:T(4,128)S(1)} %get-tuple-element.16), channel_id=1, source_target_pairs={{1,2},{2,1},{3,4},{4,3},{5,6},{6,5},{7,8},{8,7},{9,10},{10,9},{11,... | collective-permute-start | bytes 55304 | tf_op jit(solution)/shard_map/cond/branch_1_fun/ppermute | solution.py:297
  11.8 5.2 %collective-permute-start.1 = (f32[3,4,3,128]{3,2,1,0:T(4,128)S(1)}, f32[3,4,3,128]{3,2,1,0:T(4,128)}, u32[]{:S(2)}, u32[]{:S(2)}) collective-permute-start(f32[3,4,3,128]{3,2,1,0:T(4,128)S(1)} %get-tuple-element.17), channel_id=1, source_target_pairs={{0,1},{1,0},{2,3},{3,2},{4,5},{5,4},{6,7},{7,6},{8,9},{9,8},{10,11... | collective-permute-start | bytes 55304 | tf_op jit(solution)/shard_map/cond/branch_1_fun/ppermute | solution.py:297
  17.0 0.0 collective-permute-done.refs_0_
  17.0 0.9 %collective-permute-done.1.refs_1_ = f32[3,4,3,128]{3,2,1,0:T(4,128)} collective-permute-done((f32[3,4,3,128]{3,2,1,0:T(4,128)S(1)}, f32[3,4,3,128]{3,2,1,0:T(4,128)}, u32[]{:S(2)}, u32[]{:S(2)}) %collective-permute-start.1) | collective-permute-done | bytes 18464 | tf_op jit(solution)/shard_map/cond/branch_1_fun/ppermute | solution.py:297
  18.0 1.3 %collective-permute-start.6 = (f32[4,768]{1,0:T(4,128)S(1)}, f32[4,768]{1,0:T(4,128)S(1)}, u32[]{:S(2)}, u32[]{:S(2)}) collective-permute-start(f32[4,768]{1,0:T(4,128)S(1)} %after.5), channel_id=1, source_target_pairs={{65,33},{97,65},{129,97},{161,129},{193,161},{225,193},{257,225},{... | collective-permute-start | bytes 36872 | tf_op jit(solution)/shard_map/ppermute | solution.py:297
  19.3 1.1 %conditional.3 = (f32[3,4,3,128]{3,2,1,0:T(4,128)S(1)}, f32[3,4,3,128]{3,2,1,0:T(4,128)S(1)}, f32[3,4,64,128]{3,2,1,0:T(8,128)S(1)}, f32[3,4,64,128]{3,2,1,0:T(8,128)S(1)}) conditional(s32[]{:T(128)} %convert_element_type.4, (f32[3,4,3,128]{3,2,1,0:T(4,128)S(1)}, f32[3,4,3,128]{3,2,1,0:T(4,128)S(1)}, f32[3,4,64,128]{3,2,1,0:T(8,128)S(1)}, ...), branch_computations={%region_2.0_spmd, %region_3.0_spmd} | conditional | flops 600000000 | bytes 1147568 | solution.py:384
  19.3 1.1 %inner.3 = (f32[3,4,64,128]{3,2,1,0:T(8,128)S(1)}, f32[3,4,64,128]{3,2,1,0:T(8,128)S(1)}) custom-call(f32[3,4,64,128]{3,2,1,0:T(8,128)S(1)} %get-tuple-element.28.vel_ref, f32[3,4,64,128]{3,2,1,0:T(8,128)} %get-tuple-element.29.old_ref), custom_call_target="tpu_custom_call" | custom-call | flops 600000000 | bytes 1000000 | tf_op jit(solution)/shard_map/cond/branch_1_fun/inner/pallas_call | solution.py:333
  20.4 0.0 collective-permute-done.4.first_ref
  20.4 0.0 collective-permute-done.5.second_ref
  20.4 0.0 collective-permute-done.6.third_ref
  20.4 1.8 %outer.1 = (f32[3,4,64,128]{3,2,1,0:T(8,128)}, f32[3,4,64,128]{3,2,1,0:T(8,128)}) custom-call(f32[3,4,64,128]{3,2,1,0:T(8,128)S(1)} %get-tuple-element.46.vel_ref, f32[4,768]{1,0:T(4,128)S(1)} %collective-permute-done.4.first_ref, f32[4,768]{1,0:T(4,128)S(1)} %collective-permute-done.5.second_ref, f32[4,768]{1,0:T(4,128)S(1)} %collective-permute-done.6.third_ref, ...), custom_call_target="tpu_custom_call" | custom-call | tf_op jit(solution)/shard_map/outer/pallas_call | solution.py:388
  (3 shorter events, 0.0 us)
Async XLA Ops:
  2.1 18.3 %collective-permute-start.4 = (f32[4,768]{1,0:T(4,128)S(1)}, f32[4,768]{1,0:T(4,128)S(1)}, u32[]{:S(2)}, u32[]{:S(2)}) collective-permute-start(f32[4,768]{1,0:T(4,128)S(1)} %get-tuple-element.47), channel_id=1, source_target_pairs={{1,33},{33,1},{2,34},{34,2},{3,35},{35,3},{4,36},{36,4},{5,37},{37... | collective-permute-start | bytes 36872 | tf_op jit(solution)/shard_map/ppermute | solution.py:297
  6.5 13.9 %collective-permute-start.5 = (f32[4,768]{1,0:T(4,128)S(1)}, f32[4,768]{1,0:T(4,128)S(1)}, u32[]{:S(2)}, u32[]{:S(2)}) collective-permute-start(f32[4,768]{1,0:T(4,128)S(1)} %get-tuple-element.48), channel_id=1, source_target_pairs={{33,65},{65,97},{97,129},{129,161},{161,193},{193,225},{225,257},{... | collective-permute-start | bytes 36872 | tf_op jit(solution)/shard_map/ppermute | solution.py:297
  7.8 9.2 %collective-permute-start = (f32[3,4,3,128]{3,2,1,0:T(4,128)S(1)}, f32[3,4,3,128]{3,2,1,0:T(4,128)}, u32[]{:S(2)}, u32[]{:S(2)}) collective-permute-start(f32[3,4,3,128]{3,2,1,0:T(4,128)S(1)} %get-tuple-element.16), channel_id=1, source_target_pairs={{1,2},{2,1},{3,4},{4,3},{5,6},{6,5},{7,8},{8,7},{9,10},{10,9},{11,... | collective-permute-start | bytes 55304 | tf_op jit(solution)/shard_map/cond/branch_1_fun/ppermute | solution.py:297
  11.8 6.1 %collective-permute-start.1 = (f32[3,4,3,128]{3,2,1,0:T(4,128)S(1)}, f32[3,4,3,128]{3,2,1,0:T(4,128)}, u32[]{:S(2)}, u32[]{:S(2)}) collective-permute-start(f32[3,4,3,128]{3,2,1,0:T(4,128)S(1)} %get-tuple-element.17), channel_id=1, source_target_pairs={{0,1},{1,0},{2,3},{3,2},{4,5},{5,4},{6,7},{7,6},{8,9},{9,8},{10,11... | collective-permute-start | bytes 55304 | tf_op jit(solution)/shard_map/cond/branch_1_fun/ppermute | solution.py:297
  18.0 2.4 %collective-permute-start.6 = (f32[4,768]{1,0:T(4,128)S(1)}, f32[4,768]{1,0:T(4,128)S(1)}, u32[]{:S(2)}, u32[]{:S(2)}) collective-permute-start(f32[4,768]{1,0:T(4,128)S(1)} %after.5), channel_id=1, source_target_pairs={{65,33},{97,65},{129,97},{161,129},{193,161},{225,193},{257,225},{... | collective-permute-start | bytes 36872 | tf_op jit(solution)/shard_map/ppermute | solution.py:297

commit v4 on v3

--- a/solution.py
+++ b/solution.py
@@ -164,6 +164,18 @@
     return v_far * (odd * (w_near + w_far) + even)
 
 
+def lowest_kernel(vel_ref, old_ref, early_out, early_in, part_ref, base_ref, outward_ref, inward_ref, kept_ref, sem, sems):
+    moves = [
+        pltpu.make_async_copy(early_out, outward_ref, sems.at[0]),
+        pltpu.make_async_copy(early_in, inward_ref, sems.at[1]),
+    ]
+    for move in moves:
+        move.start()
+    inner_kernel(vel_ref, old_ref, part_ref, base_ref, kept_ref, sem)
+    for move in moves:
+        move.wait()
+
+
 def inner_kernel(vel_ref, old_ref, part_ref, base_ref, kept_ref, sem):
     copy = pltpu.make_async_copy(old_ref, kept_ref, sem)
     copy.start()
@@ -193,36 +205,19 @@
 
 
 def outer_kernel(
-    vel_ref, first_ref, second_ref, third_ref, part_ref, base_ref, early_out, early_in, late_out, late_in,
-    new_ref, rhs_ref, new_held, rhs_held, halos, below_ref, above_ref, sems
+    vel_ref, first_ref, second_ref, third_ref, part_ref, base_ref, outward_ref, inward_ref, early_out, early_in,
+    new_ref, rhs_ref, new_held, rhs_held, below_ref, above_ref, sems
 ):
     fields, planes, rows, cols = vel_ref.shape
     lines = planes * rows
-    lowest = lax.axis_index("gx") == 0
-    odd = lax.rem(lax.axis_index("gz"), 2) == 1
-
-    def fetch(source, slot):
-        return pltpu.make_async_copy(source, halos.at[slot], sems.at[slot])
-
-    @pl.when(lowest)
-    def _():
-        fetch(early_out, 0).start()
-        fetch(early_in, 1).start()
-
-    @pl.when(jnp.logical_not(lowest))
-    def _():
-        fetch(late_out, 0).start()
-        fetch(late_in, 1).start()
-
     below_ref[...] = jnp.zeros(below_ref.shape, jnp.float32)
     above_ref[...] = jnp.zeros(above_ref.shape, jnp.float32)
+    odd = lax.rem(lax.axis_index("gz"), 2) == 1
+    below_ref[:, :, 0:3] = jnp.where(odd, inward_ref[...], outward_ref[...])
+    above_ref[:, :, 8:11] = jnp.where(odd, outward_ref[...], inward_ref[...])
     u = vel_ref[0].reshape(lines, cols)
     gx, gz = lax.axis_index("gx"), lax.axis_index("gz")
-    even = lax.rem(gx, 2) == 0
-    first, second, third = first_ref[...], second_ref[...], third_ref[...]
-    left = jnp.where(jnp.where(gz == 0, even, gx == 1), first, second)
-    right = jnp.where(gx == lax.axis_size("gx") - 1, third, jnp.where(even, second, first))
-    right = jnp.where(gz == 0, right, jnp.where(gx == 0, first, third))
+    left, right = arrivals(gx, gz, first_ref[...], second_ref[...], third_ref[...])
     u_edge = (left[2:3, :lines], right[2:3, :lines])
     table = outer_table(cols)
     tn = (((0,), (0,)), ((), ()))
@@ -254,42 +249,41 @@
             rhs_held[i, :, at] += fix
             new_held[i, :, at] += (time_step * gamma_now) * fix
         for k, (source, target) in enumerate(((rhs_held, rhs_ref), (new_held, new_ref))):
-            copies.append(pltpu.make_async_copy(source.at[i], target.at[i], sems.at[2 + 2 * i + k]))
+            copies.append(pltpu.make_async_copy(source.at[i], target.at[i], sems.at[2 * i + k]))
             copies[-1].start()
 
-    across(0)
-    across(1)
-    fetch(early_out, 0).wait()
-    fetch(early_in, 1).wait()
-    below_ref[:, :, 0:3] = jnp.where(odd, halos[1], halos[0])
-    above_ref[:, :, 8:11] = jnp.where(odd, halos[0], halos[1])
-    along(0)
-    along(1)
-    across(2)
-    along(2)
+    for i in range(fields):
+        across(i)
+        along(i)
     for copy in copies:
         copy.wait()
 
 
 def upward_steps(gx, gz):
-    even = lax.rem(gx, 2) == 0
-    first = jnp.where(gz == 0, jnp.logical_not(even), gx == 0)
-    return first, jnp.logical_or(gz > 0, even)
+    last = lax.axis_size("gx") - 1
+    first = jnp.where(gz == 0, jnp.logical_or(gx == 1, gx == last), gx == 0)
+    return first, jnp.logical_or(gz > 0, gx != 1)
 
 
 def step_pairs(xs, zs):
     up = lambda x, z: ((x, z), ((x + 1) % xs, z))
     down = lambda x, z: ((x, z), ((x - 1) % xs, z))
-    first, second, third = [], [], []
+    first = [up(1, 0), down(2, 0), up(xs - 1, 0)] + [down(x, 0) for x in range(4, xs - 1)]
+    second = [up(0, 0), down(1, 0)] + [up(x, 0) for x in range(2, xs - 1)]
+    third = [down(3, 0), down(xs - 1, 0), down(0, 0)]
     for z in range(1, zs):
         first += [up(0, z), down(1, z)]
         second += [up(x, z) for x in range(1, xs)]
         third += [down(x, z) for x in range(2, xs)] + [down(0, z)]
-    for x in range(0, xs, 2):
-        first += [up((x - 1) % xs, 0)] + [down(x, 0)] * (x > 0)
-        second += [up(x, 0), down(x + 1, 0)]
-    third += [down(0, 0)]
     return first, second, third
+
+
+def arrivals(gx, gz, first, second, third):
+    last = lax.axis_size("gx") - 1
+    left = jnp.where(jnp.where(gz == 0, jnp.logical_or(gx == 0, gx == 2), gx == 1), first, second)
+    late = jnp.logical_or(gx == 2, gx >= last - 1)
+    column = jnp.where(gx == 0, second, jnp.where(late, third, first))
+    return left, jnp.where(gz == 0, column, jnp.where(gx == 0, first, third))
 
 
 def permute(values, pairs):
@@ -329,17 +323,19 @@
         name="moments",
     )(pltpu.with_memory_space_constraint(velocity, pltpu.HBM))
 
-    def inner(held, old):
+    def inner(held, old, *more):
+        spaces = [pltpu.VMEM, pltpu.HBM] + [pl.ANY] * len(more)
         return pl.pallas_call(
-            inner_kernel,
-            out_shape=(block, block),
-            in_specs=[whole, pl.BlockSpec(memory_space=pltpu.HBM)],
-            out_specs=(whole, whole),
-            scratch_shapes=[pltpu.VMEM(velocity.shape, f32), pltpu.SemaphoreType.DMA],
+            lowest_kernel if more else inner_kernel,
+            out_shape=(block, block) + (halo,) * len(more),
+            in_specs=[pl.BlockSpec(memory_space=x) for x in spaces],
+            out_specs=(whole,) * (2 + len(more)),
+            scratch_shapes=[pltpu.VMEM(velocity.shape, f32), pltpu.SemaphoreType.DMA]
+            + [pltpu.SemaphoreType.DMA((2,))] * bool(more),
             compiler_params=params,
             cost_estimate=pl.CostEstimate(flops=600_000_000, bytes_accessed=1_000_000, transcendentals=0),
             name="inner",
-        )(pltpu.with_memory_space_constraint(held, pltpu.VMEM), pltpu.with_memory_space_constraint(old, pltpu.HBM))
+        )(*(pltpu.with_memory_space_constraint(x, y) for x, y in zip((held, old, *more), spaces)))
 
     def unset(*shapes):
         return pl.pallas_call(
@@ -369,34 +365,33 @@
     def early_none(out, into):
         return unset(halo, halo)
 
-    def late_none(out, into, held, old):
-        return (*unset(halo, halo), *inner(held, old))
-
-    def late_swaps(out, into, held, old):
-        solved = inner(held, old)
-        return (*after((swap(out, 1, rest), swap(into, 0, rest))), *solved)
+    def late_none(out, into, early_out, early_in, held, old):
+        part, base, out, into = inner(held, old, early_out, early_in)
+        return out, into, part, base
+
+    def late_swaps(out, into, early_out, early_in, held, old):
+        part, base = inner(held, old)
+        return (*after((swap(out, 1, rest), swap(into, 0, rest))), part, base)
 
     second = permute(second, steps[1])
     first = permute(first, steps[0])
     early = lax.cond(gx == 0, early_swaps, early_none, outward, inward)
     (third,) = after((third,), *early)
     third = permute(third, steps[2])
-    late_out, late_in, part, base = lax.cond(gx == 0, late_none, late_swaps, outward, inward, held, old_rhs)
+    out, into, part, base = lax.cond(gx == 0, late_none, late_swaps, outward, inward, *early, held, old_rhs)
     scratch = pltpu.VMEM(velocity.shape, f32)
-    inputs = [held, first, second, third, part, base, *early, late_out, late_in]
-    spaces = [pltpu.VMEM] * 6 + [pl.ANY] * 4
     new_velocity, right_side = pl.pallas_call(
         outer_kernel,
         out_shape=(result, result),
-        in_specs=[pl.BlockSpec(memory_space=x) for x in spaces],
+        in_specs=[whole] * 8 + [anywhere] * 2,
         out_specs=(anywhere, anywhere),
         scratch_shapes=[
-            scratch, scratch, pltpu.VMEM((2, *halo.shape), f32),
-            *[pltpu.VMEM((fields, planes, 16, cols), f32)] * 2, pltpu.SemaphoreType.DMA((2 + 2 * fields,)),
+            scratch, scratch, *[pltpu.VMEM((fields, planes, 16, cols), f32)] * 2,
+            pltpu.SemaphoreType.DMA((2 * fields,)),
         ],
         compiler_params=params,
         name="outer",
-    )(*(pltpu.with_memory_space_constraint(x, y) for x, y in zip(inputs, spaces)))
+    )(*(pltpu.with_memory_space_constraint(x, pltpu.VMEM) for x in (held, first, second, third, part, base, out, into)), *early)
     return new_velocity, right_side
 
 

time: 22.6 us -> 21.9 us (0.969)
  Pallas kernels: 4.41 us -> 3.83 us
    pallas_call x3 -> x2, Pallas kernels: 2.91 us -> 2.32 us  [the longest x1 1.17 us: local(): pl.pallas_call(outer_kernel, out_shape=(result, result), in_specs=[whole]...]
where the time goes in v4:
time: 21.9 us; the launch traced here: 21.6 us
  starting transfers between devices  16.1 us (74%)
  Pallas kernels  3.83 us (17%)
  waiting for transfers between devices  0.96 us (4%)
  between operations  0.7 us (3%)
    ppermute x5, starting transfers between devices, permute(): lax.ppermute(values, ('gx', 'gz'), [(a * count + b, c * count + d) for (a...  16.1 us
    pallas_call x1, Pallas kernels, local(): pl.pallas_call(moments_kernel, out_shape=(block, side, side, side, halo,...  1.51 us
    pallas_call x1, Pallas kernels, local(): pl.pallas_call(outer_kernel, out_shape=(result, result), in_specs=[whole]...  1.17 us
    pallas_call x1, Pallas kernels, inner(): pl.pallas_call(lowest_kernel if more else inner_kernel, out_shape=(block,...  1.15 us
    ppermute x5, waiting for transfers between devices, permute(): lax.ppermute(values, ('gx', 'gz'), [(a * count + b, c * count + d) for (a...  0.96 us
  transfers between devices with their start and end apart: 5, of which 1 were waited for; matrix products, arithmetic and copies ran while one was open for 0% of the time, Pallas kernels for 5%

profile of v4, /device:TPU:1, one launch (start us, length us, event | category | flops | bytes accessed | tf_op | source)
XLA Modules:
  0.0 21.6 jit_solution(2417489267150039695)
XLA Ops:
  0.6 1.5 %moments.1 = (f32[3,4,64,128]{3,2,1,0:T(8,128)S(1)}, f32[4,768]{1,0:T(4,128)S(1)}, f32[4,768]{1,0:T(4,128)S(1)}, f32[4,768]{1,0:T(4,128)S(1)}, f32[3,4,3,128]{3,...) custom-call(f32[3,4,64,128]{3,2,1,0:T(8,128)} %vel_ref.1), custom_call_target="tpu_custom_call" | custom-call | tf_op jit(solution)/shard_map/moments/pallas_call | solution.py:316
  2.1 4.4 %collective-permute-start.4 = (f32[4,768]{1,0:T(4,128)S(1)}, f32[4,768]{1,0:T(4,128)S(1)}, u32[]{:S(2)}, u32[]{:S(2)}) collective-permute-start(f32[4,768]{1,0:T(4,128)S(1)} %get-tuple-element.53), channel_id=1, source_target_pairs={{32,64},{64,32},{480,0},{128,96},{160,128},{192,160},{224,192},{25... | collective-permute-start | bytes 36872 | tf_op jit(solution)/shard_map/ppermute | solution.py:291
  6.5 1.3 %collective-permute-start.5 = (f32[4,768]{1,0:T(4,128)S(1)}, f32[4,768]{1,0:T(4,128)S(1)}, u32[]{:S(2)}, u32[]{:S(2)}) collective-permute-start(f32[4,768]{1,0:T(4,128)S(1)} %get-tuple-element.54), channel_id=1, source_target_pairs={{0,32},{32,0},{64,96},{96,128},{128,160},{160,192},{192,224},{224,... | collective-permute-start | bytes 36872 | tf_op jit(solution)/shard_map/ppermute | solution.py:291
  7.8 10.1 %conditional.2 = ((f32[3,4,3,128]{3,2,1,0:T(4,128)}, f32[3,4,3,128]{3,2,1,0:T(4,128)})) conditional(s32[]{:T(128)} %convert_element_type.4, () %tuple.21, (f32[3,4,3,128]{3,2,1,0:T(4,128)S(1)}, f32[3,4,3,128]{3,2,1,0:T(4,128)S(1)}) %tuple.22), branch_computations={%region_0.0_spmd, %region_1.0_spmd} | conditional | bytes 147544 | solution.py:378
  7.8 4.0 %collective-permute-start = (f32[3,4,3,128]{3,2,1,0:T(4,128)S(1)}, f32[3,4,3,128]{3,2,1,0:T(4,128)}, u32[]{:S(2)}, u32[]{:S(2)}) collective-permute-start(f32[3,4,3,128]{3,2,1,0:T(4,128)S(1)} %get-tuple-element.20), channel_id=1, source_target_pairs={{1,2},{2,1},{3,4},{4,3},{5,6},{6,5},{7,8},{8,7},{9,10},{10,9},{11,... | collective-permute-start | bytes 55304 | tf_op jit(solution)/shard_map/cond/branch_1_fun/ppermute | solution.py:291
  11.8 5.2 %collective-permute-start.1 = (f32[3,4,3,128]{3,2,1,0:T(4,128)S(1)}, f32[3,4,3,128]{3,2,1,0:T(4,128)}, u32[]{:S(2)}, u32[]{:S(2)}) collective-permute-start(f32[3,4,3,128]{3,2,1,0:T(4,128)S(1)} %get-tuple-element.21), channel_id=1, source_target_pairs={{0,1},{1,0},{2,3},{3,2},{4,5},{5,4},{6,7},{7,6},{8,9},{9,8},{10,11... | collective-permute-start | bytes 55304 | tf_op jit(solution)/shard_map/cond/branch_1_fun/ppermute | solution.py:291
  17.0 0.0 collective-permute-done.refs_0_
  17.0 0.9 %collective-permute-done.1.refs_1_ = f32[3,4,3,128]{3,2,1,0:T(4,128)} collective-permute-done((f32[3,4,3,128]{3,2,1,0:T(4,128)S(1)}, f32[3,4,3,128]{3,2,1,0:T(4,128)}, u32[]{:S(2)}, u32[]{:S(2)}) %collective-permute-start.1) | collective-permute-done | bytes 18464 | tf_op jit(solution)/shard_map/cond/branch_1_fun/ppermute | solution.py:291
  18.0 1.3 %collective-permute-start.6 = (f32[4,768]{1,0:T(4,128)S(1)}, f32[4,768]{1,0:T(4,128)S(1)}, u32[]{:S(2)}, u32[]{:S(2)}) collective-permute-start(f32[4,768]{1,0:T(4,128)S(1)} %after.5), channel_id=1, source_target_pairs={{96,64},{480,448},{0,480},{65,33},{97,65},{129,97},{161,129},{193,... | collective-permute-start | bytes 36872 | tf_op jit(solution)/shard_map/ppermute | solution.py:291
  19.3 1.2 %conditional.3 = (f32[3,4,3,128]{3,2,1,0:T(4,128)S(1)}, f32[3,4,3,128]{3,2,1,0:T(4,128)S(1)}, f32[3,4,64,128]{3,2,1,0:T(8,128)S(1)}, f32[3,4,64,128]{3,2,1,0:T(8,128)S(1)}) conditional(s32[]{:T(128)} %convert_element_type.4, (f32[3,4,3,128]{3,2,1,0:T(4,128)S(1)}, f32[3,4,3,128]{3,2,1,0:T(4,128)S(1)}, f32[3,4,64,128]{3,2,1,0:T(8,128)S(1)}, ...), branch_computations={%region_2.0_spmd, %region_3.0_spmd} | conditional | flops 600000000 | bytes 1147568 | solution.py:381
  19.3 1.1 %inner.3 = (f32[3,4,64,128]{3,2,1,0:T(8,128)S(1)}, f32[3,4,64,128]{3,2,1,0:T(8,128)S(1)}, f32[3,4,3,128]{3,2,1,0:T(4,128)S(1)}, f32[3,4,3,128]{3,2,1,0:T(4,128)S(1)}) custom-call(f32[3,4,64,128]{3,2,1,0:T(8,128)S(1)} %get-tuple-element.30.vel_ref, f32[3,4,64,128]{3,2,1,0:T(8,128)} %get-tuple-element.31.old_ref, ...), custom_call_target="tpu_custom_call" | custom-call | flops 600000000 | bytes 1000000 | tf_op jit(solution)/shard_map/cond/branch_1_fun/inner/pallas_call | solution.py:328
  20.4 0.0 collective-permute-done.4.first_ref
  20.4 0.0 collective-permute-done.5.second_ref
  20.5 0.0 collective-permute-done.6.third_ref
  20.5 1.2 %outer.1 = (f32[3,4,64,128]{3,2,1,0:T(8,128)}, f32[3,4,64,128]{3,2,1,0:T(8,128)}) custom-call(f32[3,4,64,128]{3,2,1,0:T(8,128)S(1)} %get-tuple-element.52.vel_ref, f32[4,768]{1,0:T(4,128)S(1)} %collective-permute-done.4.first_ref, f32[4,768]{1,0:T(4,128)S(1)} %collective-permute-done.5.second_ref, f32[4,768]{1,0:T(4,128)S(1)} %collective-permute-done.6.third_ref, ...), custom_call_target="tpu_custom_call" | custom-call | tf_op jit(solution)/shard_map/outer/pallas_call | solution.py:383
  (2 shorter events, 0.0 us)
Async XLA Ops:
  2.1 18.3 %collective-permute-start.4 = (f32[4,768]{1,0:T(4,128)S(1)}, f32[4,768]{1,0:T(4,128)S(1)}, u32[]{:S(2)}, u32[]{:S(2)}) collective-permute-start(f32[4,768]{1,0:T(4,128)S(1)} %get-tuple-element.53), channel_id=1, source_target_pairs={{32,64},{64,32},{480,0},{128,96},{160,128},{192,160},{224,192},{25... | collective-permute-start | bytes 36872 | tf_op jit(solution)/shard_map/ppermute | solution.py:291
  6.5 13.9 %collective-permute-start.5 = (f32[4,768]{1,0:T(4,128)S(1)}, f32[4,768]{1,0:T(4,128)S(1)}, u32[]{:S(2)}, u32[]{:S(2)}) collective-permute-start(f32[4,768]{1,0:T(4,128)S(1)} %get-tuple-element.54), channel_id=1, source_target_pairs={{0,32},{32,0},{64,96},{96,128},{128,160},{160,192},{192,224},{224,... | collective-permute-start | bytes 36872 | tf_op jit(solution)/shard_map/ppermute | solution.py:291
  7.8 9.2 %collective-permute-start = (f32[3,4,3,128]{3,2,1,0:T(4,128)S(1)}, f32[3,4,3,128]{3,2,1,0:T(4,128)}, u32[]{:S(2)}, u32[]{:S(2)}) collective-permute-start(f32[3,4,3,128]{3,2,1,0:T(4,128)S(1)} %get-tuple-element.20), channel_id=1, source_target_pairs={{1,2},{2,1},{3,4},{4,3},{5,6},{6,5},{7,8},{8,7},{9,10},{10,9},{11,... | collective-permute-start | bytes 55304 | tf_op jit(solution)/shard_map/cond/branch_1_fun/ppermute | solution.py:291
  11.8 6.1 %collective-permute-start.1 = (f32[3,4,3,128]{3,2,1,0:T(4,128)S(1)}, f32[3,4,3,128]{3,2,1,0:T(4,128)}, u32[]{:S(2)}, u32[]{:S(2)}) collective-permute-start(f32[3,4,3,128]{3,2,1,0:T(4,128)S(1)} %get-tuple-element.21), channel_id=1, source_target_pairs={{0,1},{1,0},{2,3},{3,2},{4,5},{5,4},{6,7},{7,6},{8,9},{9,8},{10,11... | collective-permute-start | bytes 55304 | tf_op jit(solution)/shard_map/cond/branch_1_fun/ppermute | solution.py:291
  18.0 2.5 %collective-permute-start.6 = (f32[4,768]{1,0:T(4,128)S(1)}, f32[4,768]{1,0:T(4,128)S(1)}, u32[]{:S(2)}, u32[]{:S(2)}) collective-permute-start(f32[4,768]{1,0:T(4,128)S(1)} %after.5), channel_id=1, source_target_pairs={{96,64},{480,448},{0,480},{65,33},{97,65},{129,97},{161,129},{193,... | collective-permute-start | bytes 36872 | tf_op jit(solution)/shard_map/ppermute | solution.py:291

commit v5 on v4

--- a/solution.py
+++ b/solution.py
@@ -119,19 +119,19 @@
     first_up, second_up = upward_steps(gx, gz)
     nt = (((1,), (1,)), ((), ()))
 
-    def moments(values):
-        first, second = split(values)
-        got = lax.dot_general(both, first, nt, preferred_element_type=jnp.float32)
-        rest = lax.dot_general(both, second, nt, preferred_element_type=jnp.float32)
-        return got[:8] + got[8:] + rest[:8]
-
     for i in range(fields):
         for copy in copies[i]:
             copy.wait()
-        u = held_ref[0].reshape(lines, cols)
-        v = held_ref[i].reshape(lines, cols)
-        got = moments(v)
-        flux = moments(u * v)
+    u = held_ref[0].reshape(lines, cols)
+    v = held_ref[...].reshape(fields * lines, cols)
+    terms = [v] + [u * held_ref[i].reshape(lines, cols) for i in range(fields)]
+    near, rest = split(jnp.concatenate(terms, 0))
+    all_got = lax.dot_general(both, near, nt, preferred_element_type=jnp.float32)
+    rest_got = lax.dot_general(high, rest, nt, preferred_element_type=jnp.float32)
+    all_got = all_got[:8] + all_got[8:] + rest_got
+    for i in range(fields):
+        got = all_got[:, i * lines : (i + 1) * lines]
+        flux = all_got[:, (fields + i) * lines : (fields + i + 1) * lines]
         at = slice(i * lines, (i + 1) * lines)
         lower = jnp.concatenate([got[0:3], flux[0:1]], 0)
         upper = jnp.concatenate([got[3:6], flux[3:4]], 0)
@@ -162,18 +162,6 @@
     odd = -0.5 * sign * span_odd[distance - 1]
     even = viscosity * span_even[distance - 1]
     return v_far * (odd * (w_near + w_far) + even)
-
-
-def lowest_kernel(vel_ref, old_ref, early_out, early_in, part_ref, base_ref, outward_ref, inward_ref, kept_ref, sem, sems):
-    moves = [
-        pltpu.make_async_copy(early_out, outward_ref, sems.at[0]),
-        pltpu.make_async_copy(early_in, inward_ref, sems.at[1]),
-    ]
-    for move in moves:
-        move.start()
-    inner_kernel(vel_ref, old_ref, part_ref, base_ref, kept_ref, sem)
-    for move in moves:
-        move.wait()
 
 
 def inner_kernel(vel_ref, old_ref, part_ref, base_ref, kept_ref, sem):
@@ -204,20 +192,68 @@
         base_ref[i] = vel_ref[i] + fresh
 
 
+def set_margins(outward, inward, below_ref, above_ref):
+    odd = lax.rem(lax.axis_index("gz"), 2) == 1
+    below_ref[...] = jnp.zeros(below_ref.shape, jnp.float32)
+    above_ref[...] = jnp.zeros(above_ref.shape, jnp.float32)
+    below_ref[:, :, 0:3] = jnp.where(odd, inward, outward)
+    above_ref[:, :, 8:11] = jnp.where(odd, outward, inward)
+
+
+def edge_terms(vel_ref, below_ref, above_ref, i):
+    rows = vel_ref.shape[2]
+    w_low, w_high = vel_ref[2, :, 0:8], vel_ref[2, :, rows - 8 :]
+    low, high = 0.0, 0.0
+    for d in (1, 2, 3):
+        near = slice(3 - d, 11 - d)
+        low = low + span_tap(below_ref[i, :, near], w_low, below_ref[2, :, near], d, -1)
+        near = slice(d, d + 8)
+        high = high + span_tap(above_ref[i, :, near], w_high, above_ref[2, :, near], d, 1)
+    return low, high
+
+
+def edges_kernel(vel_ref, outward_ref, inward_ref, edges_ref, below_ref, above_ref):
+    set_margins(outward_ref[...], inward_ref[...], below_ref, above_ref)
+    for i in range(vel_ref.shape[0]):
+        edges_ref[i, :, 0:8], edges_ref[i, :, 8:16] = edge_terms(vel_ref, below_ref, above_ref, i)
+
+
+def lowest_kernel(
+    vel_ref, first_ref, second_ref, part_ref, base_ref, edges_ref, late_ref,
+    new_ref, rhs_ref, new_held, rhs_held, sems
+):
+    @pl.when(lax.axis_index("gx") == 0)
+    def _():
+        finish(
+            vel_ref, first_ref, second_ref, None, part_ref, base_ref,
+            lambda i: (edges_ref[i, :, 0:8], edges_ref[i, :, 8:16]),
+            new_ref, rhs_ref, new_held, rhs_held, sems
+        )
+
+
 def outer_kernel(
-    vel_ref, first_ref, second_ref, third_ref, part_ref, base_ref, outward_ref, inward_ref, early_out, early_in,
+    vel_ref, first_ref, second_ref, third_ref, part_ref, base_ref, outward_ref, inward_ref, new_before, rhs_before,
     new_ref, rhs_ref, new_held, rhs_held, below_ref, above_ref, sems
+):
+    @pl.when(lax.axis_index("gx") > 0)
+    def _():
+        set_margins(outward_ref[...], inward_ref[...], below_ref, above_ref)
+        finish(
+            vel_ref, first_ref, second_ref, third_ref, part_ref, base_ref,
+            functools.partial(edge_terms, vel_ref, below_ref, above_ref),
+            new_ref, rhs_ref, new_held, rhs_held, sems
+        )
+
+
+def finish(
+    vel_ref, first_ref, second_ref, third_ref, part_ref, base_ref, edges,
+    new_ref, rhs_ref, new_held, rhs_held, sems
 ):
     fields, planes, rows, cols = vel_ref.shape
     lines = planes * rows
-    below_ref[...] = jnp.zeros(below_ref.shape, jnp.float32)
-    above_ref[...] = jnp.zeros(above_ref.shape, jnp.float32)
-    odd = lax.rem(lax.axis_index("gz"), 2) == 1
-    below_ref[:, :, 0:3] = jnp.where(odd, inward_ref[...], outward_ref[...])
-    above_ref[:, :, 8:11] = jnp.where(odd, outward_ref[...], inward_ref[...])
     u = vel_ref[0].reshape(lines, cols)
     gx, gz = lax.axis_index("gx"), lax.axis_index("gz")
-    left, right = arrivals(gx, gz, first_ref[...], second_ref[...], third_ref[...])
+    left, right = arrivals(gx, gz, first_ref[...], second_ref[...], None if third_ref is None else third_ref[...])
     u_edge = (left[2:3, :lines], right[2:3, :lines])
     table = outer_table(cols)
     tn = (((0,), (0,)), ((), ()))
@@ -238,13 +274,7 @@
         new_held[i] = base_ref[i] + (time_step * gamma_now) * extra
 
     def along(i):
-        w_low, w_high = vel_ref[2, :, 0:8], vel_ref[2, :, rows - 8 :]
-        low_fix, high_fix = 0.0, 0.0
-        for d in (1, 2, 3):
-            near = slice(3 - d, 11 - d)
-            low_fix = low_fix + span_tap(below_ref[i, :, near], w_low, below_ref[2, :, near], d, -1)
-            near = slice(d, d + 8)
-            high_fix = high_fix + span_tap(above_ref[i, :, near], w_high, above_ref[2, :, near], d, 1)
+        low_fix, high_fix = edges(i)
         for at, fix in ((slice(0, 8), low_fix), (slice(rows - 8, rows), high_fix)):
             rhs_held[i, :, at] += fix
             new_held[i, :, at] += (time_step * gamma_now) * fix
@@ -281,6 +311,8 @@
 def arrivals(gx, gz, first, second, third):
     last = lax.axis_size("gx") - 1
     left = jnp.where(jnp.where(gz == 0, jnp.logical_or(gx == 0, gx == 2), gx == 1), first, second)
+    if third is None:
+        return left, jnp.where(gz == 0, second, first)
     late = jnp.logical_or(gx == 2, gx >= last - 1)
     column = jnp.where(gx == 0, second, jnp.where(late, third, first))
     return left, jnp.where(gz == 0, column, jnp.where(gx == 0, first, third))
@@ -310,6 +342,8 @@
     block = pltpu.VMEM(velocity.shape, f32)
     side = pltpu.VMEM((4, fields * lines), f32)
     halo = pltpu.VMEM((fields, planes, 3, cols), f32)
+    edge = pltpu.VMEM((fields, planes, 16, cols), f32)
+    margins = edge
     result = jax.ShapeDtypeStruct(velocity.shape, f32)
     params = pltpu.CompilerParams(vmem_limit_bytes=32 * 1024 * 1024)
 
@@ -323,19 +357,17 @@
         name="moments",
     )(pltpu.with_memory_space_constraint(velocity, pltpu.HBM))
 
-    def inner(held, old, *more):
-        spaces = [pltpu.VMEM, pltpu.HBM] + [pl.ANY] * len(more)
+    def inner(held, old):
         return pl.pallas_call(
-            lowest_kernel if more else inner_kernel,
-            out_shape=(block, block) + (halo,) * len(more),
-            in_specs=[pl.BlockSpec(memory_space=x) for x in spaces],
-            out_specs=(whole,) * (2 + len(more)),
-            scratch_shapes=[pltpu.VMEM(velocity.shape, f32), pltpu.SemaphoreType.DMA]
-            + [pltpu.SemaphoreType.DMA((2,))] * bool(more),
+            inner_kernel,
+            out_shape=(block, block),
+            in_specs=[whole, pl.BlockSpec(memory_space=pltpu.HBM)],
+            out_specs=(whole, whole),
+            scratch_shapes=[pltpu.VMEM(velocity.shape, f32), pltpu.SemaphoreType.DMA],
             compiler_params=params,
             cost_estimate=pl.CostEstimate(flops=600_000_000, bytes_accessed=1_000_000, transcendentals=0),
             name="inner",
-        )(*(pltpu.with_memory_space_constraint(x, y) for x, y in zip((held, old, *more), spaces)))
+        )(pltpu.with_memory_space_constraint(held, pltpu.VMEM), pltpu.with_memory_space_constraint(old, pltpu.HBM))
 
     def unset(*shapes):
         return pl.pallas_call(
@@ -359,39 +391,58 @@
     steps = step_pairs(xs, zs)
     rest = range(1, xs)
 
-    def early_swaps(out, into):
-        return after((swap(out, 1, [0]), swap(into, 0, [0])))
-
-    def early_none(out, into):
-        return unset(halo, halo)
-
-    def late_none(out, into, early_out, early_in, held, old):
-        part, base, out, into = inner(held, old, early_out, early_in)
-        return out, into, part, base
-
-    def late_swaps(out, into, early_out, early_in, held, old):
+    def early_swaps(out, into, held, old):
+        part, base = inner(held, old)
+        arrays = (held, swap(out, 1, [0]), swap(into, 0, [0]))
+        terms = pl.pallas_call(
+            edges_kernel,
+            out_shape=edge,
+            in_specs=[whole] * 3,
+            out_specs=whole,
+            scratch_shapes=[margins, margins],
+            compiler_params=params,
+            name="edges",
+        )(*(pltpu.with_memory_space_constraint(x, pltpu.VMEM) for x in arrays))
+        return terms, part, base
+
+    def early_none(out, into, held, old):
+        return unset(edge, block, block)
+
+    def late_swaps(out, into, held, old):
         part, base = inner(held, old)
         return (*after((swap(out, 1, rest), swap(into, 0, rest))), part, base)
 
+    def none(out, into, held, old):
+        return unset(halo, halo, block, block)
+
     second = permute(second, steps[1])
     first = permute(first, steps[0])
-    early = lax.cond(gx == 0, early_swaps, early_none, outward, inward)
-    (third,) = after((third,), *early)
+    early = lax.cond(gx == 0, early_swaps, early_none, outward, inward, held, old_rhs)
+    (third,) = after((third,), early[0])
     third = permute(third, steps[2])
-    out, into, part, base = lax.cond(gx == 0, late_none, late_swaps, outward, inward, *early, held, old_rhs)
+    late = lax.cond(gx == 0, none, late_swaps, outward, inward, held, old_rhs)
     scratch = pltpu.VMEM(velocity.shape, f32)
-    new_velocity, right_side = pl.pallas_call(
-        outer_kernel,
-        out_shape=(result, result),
-        in_specs=[whole] * 8 + [anywhere] * 2,
-        out_specs=(anywhere, anywhere),
-        scratch_shapes=[
-            scratch, scratch, *[pltpu.VMEM((fields, planes, 16, cols), f32)] * 2,
-            pltpu.SemaphoreType.DMA((2 * fields,)),
-        ],
-        compiler_params=params,
-        name="outer",
-    )(*(pltpu.with_memory_space_constraint(x, pltpu.VMEM) for x in (held, first, second, third, part, base, out, into)), *early)
+    sems = pltpu.SemaphoreType.DMA((2 * fields,))
+
+    def last(kernel, arrays, loose, scratches, **more):
+        spaces = [pltpu.VMEM] * len(arrays) + [pl.ANY] * len(loose)
+        return pl.pallas_call(
+            kernel,
+            out_shape=(result, result),
+            in_specs=[pl.BlockSpec(memory_space=x) for x in spaces],
+            out_specs=(anywhere, anywhere),
+            scratch_shapes=scratches,
+            compiler_params=params,
+            **more,
+        )(*(pltpu.with_memory_space_constraint(x, pltpu.VMEM) for x in arrays), *loose)
+
+    before = last(
+        lowest_kernel, (held, first, second, *early[1:], early[0]), (late[0],), [scratch, scratch, sems], name="lowest",
+    )
+    new_velocity, right_side = last(
+        outer_kernel, (held, first, second, third, *late[2:], *late[:2]), before,
+        [scratch, scratch, margins, margins, sems], name="outer", input_output_aliases={8: 0, 9: 1},
+    )
     return new_velocity, right_side
 
 

time: 21.9 us -> 21.5 us (0.982)
  the two profiles are of different devices: /device:TPU:1 before, /device:TPU:32 now
where the time goes in v5:
time: 21.5 us; the launch traced here: 21.3 us
  starting transfers between devices  14 us (65%)
  Pallas kernels  3.76 us (17%)
  waiting for transfers between devices  2.72 us (13%)
  between operations  0.73 us (3%)
    ppermute x5, starting transfers between devices, permute(): lax.ppermute(values, ('gx', 'gz'), [(a * count + b, c * count + d) for (a...  14 us
    ppermute x5, waiting for transfers between devices, permute(): lax.ppermute(values, ('gx', 'gz'), [(a * count + b, c * count + d) for (a...  2.72 us
    pallas_call x1, Pallas kernels, local(): pl.pallas_call(moments_kernel, out_shape=(block, side, side, side, halo,...  1.42 us
    pallas_call x2, Pallas kernels, last(): pl.pallas_call(kernel, out_shape=(result, result), in_specs=[pl.BlockSpec...  1.25 us
    pallas_call x1, Pallas kernels, inner(): pl.pallas_call(inner_kernel, out_shape=(block, block), in_specs=[whole, p...  1.09 us
  transfers between devices with their start and end apart: 5, of which 1 were waited for; matrix products, arithmetic and copies ran while one was open for 0% of the time, Pallas kernels for 5%

profile of v5, /device:TPU:32, one launch (start us, length us, event | category | flops | bytes accessed | tf_op | source)
XLA Modules:
  0.0 21.3 jit_solution(12502670850620648641)
XLA Ops:
  0.6 0.0 copy-start
  0.6 1.4 %moments.1 = (f32[3,4,64,128]{3,2,1,0:T(8,128)S(1)}, f32[4,768]{1,0:T(4,128)S(1)}, f32[4,768]{1,0:T(4,128)S(1)}, f32[4,768]{1,0:T(4,128)S(1)}, f32[3,4,3,128]{3,...) custom-call(f32[3,4,64,128]{3,2,1,0:T(8,128)} %vel_ref.1), custom_call_target="tpu_custom_call" | custom-call | tf_op jit(solution)/shard_map/moments/pallas_call | solution.py:350
  2.1 3.8 %collective-permute-start.4 = (f32[4,768]{1,0:T(4,128)S(1)}, f32[4,768]{1,0:T(4,128)S(1)}, u32[]{:S(2)}, u32[]{:S(2)}) collective-permute-start(f32[4,768]{1,0:T(4,128)S(1)} %get-tuple-element.48), channel_id=1, source_target_pairs={{32,64},{64,32},{480,0},{128,96},{160,128},{192,160},{224,192},{25... | collective-permute-start | bytes 36872 | tf_op jit(solution)/shard_map/ppermute | solution.py:323
  5.9 4.9 %collective-permute-start.5 = (f32[4,768]{1,0:T(4,128)S(1)}, f32[4,768]{1,0:T(4,128)S(1)}, u32[]{:S(2)}, u32[]{:S(2)}) collective-permute-start(f32[4,768]{1,0:T(4,128)S(1)} %get-tuple-element.49), channel_id=1, source_target_pairs={{0,32},{32,0},{64,96},{96,128},{128,160},{160,192},{192,224},{224,... | collective-permute-start | bytes 36872 | tf_op jit(solution)/shard_map/ppermute | solution.py:323
  10.8 0.0 copy-done
  10.8 0.7 %collective-permute-start.6 = (f32[4,768]{1,0:T(4,128)S(1)}, f32[4,768]{1,0:T(4,128)S(1)}, u32[]{:S(2)}, u32[]{:S(2)}) collective-permute-start(f32[4,768]{1,0:T(4,128)S(1)} %after.3), channel_id=1, source_target_pairs={{96,64},{480,448},{0,480},{65,33},{97,65},{129,97},{161,129},{193,... | collective-permute-start | bytes 36872 | tf_op jit(solution)/shard_map/ppermute | solution.py:323
  11.5 8.5 %conditional.3 = ((f32[3,4,3,128]{3,2,1,0:T(4,128)S(1)}, f32[3,4,3,128]{3,2,1,0:T(4,128)S(1)}, f32[3,4,64,128]{3,2,1,0:T(8,128)S(1)}, f32[3,4,64,128]{3,2,1,0:T(8,128)S(1)})) conditional(s32[]{:T(128)} %convert_element_type.4, (f32[3,4,3,128]{3,2,1,0:T(4,128)S(1)}, f32[3,4,3,128]{3,2,1,0:T(4,128)S(1)}, f32[3,4,64,128]{3,2,1,0:T(8,128)S(1)}, ...), branch_computations={%region_2.0_spmd, %region_3.0_spmd} | conditional | flops 600000000 | bytes 2720468 | solution.py:423
  11.5 0.0 copy-start.1
  11.5 2.7 %collective-permute-start.2 = (f32[3,4,3,128]{3,2,1,0:T(4,128)S(1)}, f32[3,4,3,128]{3,2,1,0:T(4,128)S(1)}, u32[]{:S(2)}, u32[]{:S(2)}) collective-permute-start(f32[3,4,3,128]{3,2,1,0:T(4,128)S(1)} %get-tuple-element.22), channel_id=1, source_target_pairs={{33,34},{34,33},{35,36},{36,35},{37,38},{38,37},{39,40},{40,39},{4... | collective-permute-start | bytes 55304 | tf_op jit(solution)/shard_map/cond/branch_0_fun/ppermute | solution.py:323
  14.2 1.9 %collective-permute-start.3 = (f32[3,4,3,128]{3,2,1,0:T(4,128)S(1)}, f32[3,4,3,128]{3,2,1,0:T(4,128)S(1)}, u32[]{:S(2)}, u32[]{:S(2)}) collective-permute-start(f32[3,4,3,128]{3,2,1,0:T(4,128)S(1)} %get-tuple-element.23), channel_id=1, source_target_pairs={{32,33},{33,32},{34,35},{35,34},{36,37},{37,36},{38,39},{39,38},{4... | collective-permute-start | bytes 55304 | tf_op jit(solution)/shard_map/cond/branch_0_fun/ppermute | solution.py:323
  16.2 0.0 copy-done.1
  16.2 1.1 %inner.3 = (f32[3,4,64,128]{3,2,1,0:T(8,128)S(1)}, f32[3,4,64,128]{3,2,1,0:T(8,128)S(1)}) custom-call(f32[3,4,64,128]{3,2,1,0:T(8,128)S(1)} %get-tuple-element.26.vel_ref, f32[3,4,64,128]{3,2,1,0:T(8,128)} %copy-done.1), custom_call_target="tpu_custom_call" | custom-call | flops 600000000 | bytes 1000000 | tf_op jit(solution)/shard_map/cond/branch_0_fun/inner/pallas_call | solution.py:361
  17.3 2.7 %collective-permute-done.2.refs_0_ = f32[3,4,3,128]{3,2,1,0:T(4,128)S(1)} collective-permute-done((f32[3,4,3,128]{3,2,1,0:T(4,128)S(1)}, f32[3,4,3,128]{3,2,1,0:T(4,128)S(1)}, u32[]{:S(2)}, u32[]{:S(2)}) %collective-permute-start.2) | collective-permute-done | bytes 18464 | tf_op jit(solution)/shard_map/cond/branch_0_fun/ppermute | solution.py:323
  20.0 0.0 collective-permute-done.3.refs_1_
  20.0 0.0 collective-permute-done.4.first_ref
  20.0 0.0 collective-permute-done.5.second_ref
  20.0 0.1 lowest.1
  20.1 0.0 collective-permute-done.6.third_ref
  20.1 1.2 %outer.1 = (f32[3,4,64,128]{3,2,1,0:T(8,128)}, f32[3,4,64,128]{3,2,1,0:T(8,128)}) custom-call(f32[3,4,64,128]{3,2,1,0:T(8,128)S(1)} %get-tuple-element.47.vel_ref, f32[4,768]{1,0:T(4,128)S(1)} %collective-permute-done.4.first_ref, f32[4,768]{1,0:T(4,128)S(1)} %collective-permute-done.5.second_ref, ...), custom_call_target="tpu_custom_call", output_to_operand_aliasing={{0}: (8, {}), {1}: (9, {})} | custom-call | tf_op jit(solution)/shard_map/outer/pallas_call | solution.py:429
  (4 shorter events, 0.0 us)
Async XLA Ops:
  0.6 10.1 %copy-start = (f32[3,4,64,128]{3,2,1,0:T(8,128)S(1)}, f32[3,4,64,128]{3,2,1,0:T(8,128)}, u32[]{:S(2)}) copy-start(f32[3,4,64,128]{3,2,1,0:T(8,128)} %param.7) | copy-start | bytes 1179652
  2.1 17.9 %collective-permute-start.4 = (f32[4,768]{1,0:T(4,128)S(1)}, f32[4,768]{1,0:T(4,128)S(1)}, u32[]{:S(2)}, u32[]{:S(2)}) collective-permute-start(f32[4,768]{1,0:T(4,128)S(1)} %get-tuple-element.48), channel_id=1, source_target_pairs={{32,64},{64,32},{480,0},{128,96},{160,128},{192,160},{224,192},{25... | collective-permute-start | bytes 36872 | tf_op jit(solution)/shard_map/ppermute | solution.py:323
  5.9 14.1 %collective-permute-start.5 = (f32[4,768]{1,0:T(4,128)S(1)}, f32[4,768]{1,0:T(4,128)S(1)}, u32[]{:S(2)}, u32[]{:S(2)}) collective-permute-start(f32[4,768]{1,0:T(4,128)S(1)} %get-tuple-element.49), channel_id=1, source_target_pairs={{0,32},{32,0},{64,96},{96,128},{128,160},{160,192},{192,224},{224,... | collective-permute-start | bytes 36872 | tf_op jit(solution)/shard_map/ppermute | solution.py:323
  10.8 9.3 %collective-permute-start.6 = (f32[4,768]{1,0:T(4,128)S(1)}, f32[4,768]{1,0:T(4,128)S(1)}, u32[]{:S(2)}, u32[]{:S(2)}) collective-permute-start(f32[4,768]{1,0:T(4,128)S(1)} %after.3), channel_id=1, source_target_pairs={{96,64},{480,448},{0,480},{65,33},{97,65},{129,97},{161,129},{193,... | collective-permute-start | bytes 36872 | tf_op jit(solution)/shard_map/ppermute | solution.py:323
  11.5 4.7 %copy-start.1 = (f32[3,4,64,128]{3,2,1,0:T(8,128)}, f32[3,4,64,128]{3,2,1,0:T(8,128)S(1)}, u32[]{:S(2)}) copy-start(f32[3,4,64,128]{3,2,1,0:T(8,128)S(1)} %get-tuple-element.27.old_ref) | copy-start | bytes 1179652 | tf_op jit(solution)/shard_map/cond
  11.5 8.5 %collective-permute-start.2 = (f32[3,4,3,128]{3,2,1,0:T(4,128)S(1)}, f32[3,4,3,128]{3,2,1,0:T(4,128)S(1)}, u32[]{:S(2)}, u32[]{:S(2)}) collective-permute-start(f32[3,4,3,128]{3,2,1,0:T(4,128)S(1)} %get-tuple-element.22), channel_id=1, source_target_pairs={{33,34},{34,33},{35,36},{36,35},{37,38},{38,37},{39,40},{40,39},{4... | collective-permute-start | bytes 55304 | tf_op jit(solution)/shard_map/cond/branch_0_fun/ppermute | solution.py:323
  14.2 5.8 %collective-permute-start.3 = (f32[3,4,3,128]{3,2,1,0:T(4,128)S(1)}, f32[3,4,3,128]{3,2,1,0:T(4,128)S(1)}, u32[]{:S(2)}, u32[]{:S(2)}) collective-permute-start(f32[3,4,3,128]{3,2,1,0:T(4,128)S(1)} %get-tuple-element.23), channel_id=1, source_target_pairs={{32,33},{33,32},{34,35},{35,34},{36,37},{37,36},{38,39},{39,38},{4... | collective-permute-start | bytes 55304 | tf_op jit(solution)/shard_map/cond/branch_0_fun/ppermute | solution.py:323

commit v6 on v5

--- a/solution.py
+++ b/solution.py
@@ -116,7 +116,9 @@
     both = jnp.concatenate([high, low], 0)
     gx, gz = lax.axis_index("gx"), lax.axis_index("gz")
     odd = lax.rem(gz, 2)
-    first_up, second_up = upward_steps(gx, gz)
+    xs, zs = lax.axis_size("gx"), lax.axis_size("gz")
+    ups = upward_steps(gx, gz, xs, zs)
+    inward_first, outward_third = place_of(gx, gz, xs, zs)
     nt = (((1,), (1,)), ((), ()))
 
     for i in range(fields):
@@ -135,12 +137,24 @@
         at = slice(i * lines, (i + 1) * lines)
         lower = jnp.concatenate([got[0:3], flux[0:1]], 0)
         upper = jnp.concatenate([got[3:6], flux[3:4]], 0)
-        first_ref[:, at] = jnp.where(first_up, upper, lower)
-        second_ref[:, at] = jnp.where(second_up, upper, lower)
-        third_ref[:, at] = lower
+        for row in range(4):
+            for half in range(2):
+                near = slice(half * cols, (half + 1) * cols)
+                below, above = lower[row : row + 1, near], upper[row : row + 1, near]
+                first_ref[i, row, half : half + 1] = jnp.where(ups[0], above, below)
+                second_ref[i, row, half : half + 1] = jnp.where(ups[1], above, below)
+                third_ref[i, row, half : half + 1] = below
         head, tail = held_ref[i, :, :3], held_ref[i, :, rows - 3 :]
         inward_ref[i] = jnp.where(odd == 0, tail, head)
         outward_ref[i] = jnp.where(odd == 0, head, tail)
+
+    @pl.when(outward_third)
+    def _():
+        third_ref[...] = outward_ref[...]
+
+    @pl.when(inward_first)
+    def _():
+        first_ref[...] = inward_ref[...]
 
 
 def mul_split(values, table):
@@ -237,7 +251,11 @@
 ):
     @pl.when(lax.axis_index("gx") > 0)
     def _():
-        set_margins(outward_ref[...], inward_ref[...], below_ref, above_ref)
+        gx, gz = lax.axis_index("gx"), lax.axis_index("gz")
+        inward_first, outward_third = place_of(gx, gz, lax.axis_size("gx"), lax.axis_size("gz"))
+        outward = jnp.where(outward_third, third_ref[...], outward_ref[...])
+        inward = jnp.where(inward_first, first_ref[...], inward_ref[...])
+        set_margins(outward, inward, below_ref, above_ref)
         finish(
             vel_ref, first_ref, second_ref, third_ref, part_ref, base_ref,
             functools.partial(edge_terms, vel_ref, below_ref, above_ref),
@@ -253,7 +271,9 @@
     lines = planes * rows
     u = vel_ref[0].reshape(lines, cols)
     gx, gz = lax.axis_index("gx"), lax.axis_index("gz")
-    left, right = arrivals(gx, gz, first_ref[...], second_ref[...], None if third_ref is None else third_ref[...])
+    xs, zs = lax.axis_size("gx"), lax.axis_size("gz")
+    third = None if third_ref is None else gathered(third_ref)
+    left, right = arrivals(gx, gz, xs, zs, gathered(first_ref), gathered(second_ref), third)
     u_edge = (left[2:3, :lines], right[2:3, :lines])
     table = outer_table(cols)
     tn = (((0,), (0,)), ((), ()))
@@ -289,33 +309,56 @@
         copy.wait()
 
 
-def upward_steps(gx, gz):
-    last = lax.axis_size("gx") - 1
-    first = jnp.where(gz == 0, jnp.logical_or(gx == 1, gx == last), gx == 0)
-    return first, jnp.logical_or(gz > 0, gx != 1)
+def place_of(gx, gz, xs, zs):
+    inward = jnp.logical_and(gz <= 1, jnp.logical_and(gx >= 3, gx <= xs - 2))
+    outward = jnp.logical_and(jnp.logical_or(gz == 0, gz == zs - 1), gx == 1)
+    return inward, outward
+
+
+def upward_steps(gx, gz, xs, zs):
+    low, top = gz == 0, gz == zs - 1
+    first = jnp.where(low, jnp.logical_or(gx == 1, gx == xs - 1), jnp.logical_or(top, gx == 0))
+    down = jnp.logical_or(jnp.logical_and(low, gx == 1), jnp.logical_and(top, jnp.logical_or(gx == 1, gx == 2)))
+    return first, jnp.logical_not(down)
 
 
 def step_pairs(xs, zs):
     up = lambda x, z: ((x, z), ((x + 1) % xs, z))
     down = lambda x, z: ((x, z), ((x - 1) % xs, z))
-    first = [up(1, 0), down(2, 0), up(xs - 1, 0)] + [down(x, 0) for x in range(4, xs - 1)]
-    second = [up(0, 0), down(1, 0)] + [up(x, 0) for x in range(2, xs - 1)]
-    third = [down(3, 0), down(xs - 1, 0), down(0, 0)]
-    for z in range(1, zs):
+    top = zs - 1
+    first = [up(1, 0), down(2, 0), up(xs - 1, 0)] + [up(x, top) for x in (0, 1, 2, xs - 1)]
+    second = [up(0, 0), down(1, 0), down(1, top), down(2, top)]
+    second += [up(x, 0) for x in range(2, xs - 1)] + [up(x, top) for x in range(3, xs - 1)]
+    third = [down(x, z) for z in (0, top) for x in (0, *range(3, xs))]
+    for z in range(1, top):
         first += [up(0, z), down(1, z)]
         second += [up(x, z) for x in range(1, xs)]
         third += [down(x, z) for x in range(2, xs)] + [down(0, z)]
+    for x in range(3, xs - 1):
+        first += [((x, 0), (x, 1)), ((x, 1), (x, 0))]
+    third += [((1, 0), (1, top)), ((1, top), (1, 0))]
     return first, second, third
 
 
-def arrivals(gx, gz, first, second, third):
-    last = lax.axis_size("gx") - 1
-    left = jnp.where(jnp.where(gz == 0, jnp.logical_or(gx == 0, gx == 2), gx == 1), first, second)
+def arrivals(gx, gz, xs, zs, first, second, third):
+    low, top = gz == 0, gz == zs - 1
     if third is None:
-        return left, jnp.where(gz == 0, second, first)
-    late = jnp.logical_or(gx == 2, gx >= last - 1)
-    column = jnp.where(gx == 0, second, jnp.where(late, third, first))
-    return left, jnp.where(gz == 0, column, jnp.where(gx == 0, first, third))
+        side = jnp.logical_or(low, top)
+        return jnp.where(side, first, second), jnp.where(side, second, first)
+    left = jnp.where(jnp.where(low, gx == 2, jnp.where(top, gx <= 3, gx == 1)), first, second)
+    right = jnp.where(jnp.logical_and(low, gx == 1), first, third)
+    return left, jnp.where(jnp.logical_and(top, gx == 1), second, right)
+
+
+def gathered(ref):
+    fields = ref.shape[0]
+    return jnp.concatenate(
+        [
+            jnp.concatenate([ref[i, row, half : half + 1] for i in range(fields) for half in range(2)], 1)
+            for row in range(4)
+        ],
+        0,
+    )
 
 
 def permute(values, pairs):
@@ -323,13 +366,14 @@
     return lax.ppermute(values, ("gx", "gz"), [(a * count + b, c * count + d) for (a, b), (c, d) in pairs])
 
 
-def swap(values, first, blocks):
+def swap(values, first, blocks, done=()):
     count = lax.axis_size("gz")
     pairs = []
     for x in blocks:
         for i in range(count // 2):
             a, b = ((x, (2 * i + k + first) % count) for k in (0, 1))
-            pairs += [(a, b), (b, a)]
+            if x not in done or (a[1] > 0 and b[1] > 0):
+                pairs += [(a, b), (b, a)]
     return permute(values, pairs)
 
 
@@ -349,7 +393,7 @@
 
     held, first, second, third, outward, inward = pl.pallas_call(
         moments_kernel,
-        out_shape=(block, side, side, side, halo, halo),
+        out_shape=(block, halo, halo, halo, halo, halo),
         in_specs=[pl.BlockSpec(memory_space=pltpu.HBM)],
         out_specs=(whole,) * 6,
         scratch_shapes=[pltpu.SemaphoreType.DMA((fields * planes,))],
@@ -410,7 +454,7 @@
 
     def late_swaps(out, into, held, old):
         part, base = inner(held, old)
-        return (*after((swap(out, 1, rest), swap(into, 0, rest))), part, base)
+        return (*after((swap(out, 1, rest, (1,)), swap(into, 0, rest, range(3, xs - 1)))), part, base)
 
     def none(out, into, held, old):
         return unset(halo, halo, block, block)

time: 21.5 us -> 21.2 us (0.986)
  the two profiles are of different devices: /device:TPU:32 before, /device:TPU:1 now
where the time goes in v6:
time: 21.2 us; the launch traced here: 20.9 us
  starting transfers between devices  16.1 us (76%)
  Pallas kernels  3.94 us (19%)
  between operations  0.74 us (3%)
    ppermute x5, starting transfers between devices, permute(): lax.ppermute(values, ('gx', 'gz'), [(a * count + b, c * count + d) for (a...  16.1 us
    pallas_call x1, Pallas kernels, local(): pl.pallas_call(moments_kernel, out_shape=(block, halo, halo, halo, halo,...  1.43 us
    pallas_call x2, Pallas kernels, last(): pl.pallas_call(kernel, out_shape=(result, result), in_specs=[pl.BlockSpec...  1.24 us
    pallas_call x1, Pallas kernels, inner(): pl.pallas_call(inner_kernel, out_shape=(block, block), in_specs=[whole, p...  1.2 us
  transfers between devices with their start and end apart: 5, of which 0 were waited for; matrix products, arithmetic and copies ran while one was open for 0% of the time, Pallas kernels for 12%

profile of v6, /device:TPU:1, one launch (start us, length us, event | category | flops | bytes accessed | tf_op | source)
XLA Modules:
  0.0 20.9 jit_solution(13272917480150942672)
XLA Ops:
  0.6 0.0 copy-start
  0.6 1.4 %moments.1 = (f32[3,4,64,128]{3,2,1,0:T(8,128)S(1)}, f32[3,4,3,128]{3,2,1,0:T(4,128)S(1)}, f32[3,4,3,128]{3,2,1,0:T(4,128)S(1)}, f32[3,4,3,128]{3,2,1,0:T(4,128)...) custom-call(f32[3,4,64,128]{3,2,1,0:T(8,128)} %vel_ref.1), custom_call_target="tpu_custom_call" | custom-call | tf_op jit(solution)/shard_map/moments/pallas_call | solution.py:394
  2.1 4.4 %collective-permute-start.4 = (f32[3,4,3,128]{3,2,1,0:T(4,128)S(1)}, f32[3,4,3,128]{3,2,1,0:T(4,128)S(1)}, u32[]{:S(2)}, u32[]{:S(2)}) collective-permute-start(f32[3,4,3,128]{3,2,1,0:T(4,128)S(1)} %get-tuple-element.48), channel_id=1, source_target_pairs={{32,64},{64,32},{480,0},{31,63},{63,95},{95,127},{511,31},{1,33},{... | collective-permute-start | bytes 55304 | tf_op jit(solution)/shard_map/ppermute | solution.py:366
  6.5 1.3 %collective-permute-start.5 = (f32[3,4,3,128]{3,2,1,0:T(4,128)S(1)}, f32[3,4,3,128]{3,2,1,0:T(4,128)S(1)}, u32[]{:S(2)}, u32[]{:S(2)}) collective-permute-start(f32[3,4,3,128]{3,2,1,0:T(4,128)S(1)} %get-tuple-element.49), channel_id=1, source_target_pairs={{0,32},{32,0},{63,31},{95,63},{64,96},{96,128},{128,160},{160,192}... | collective-permute-start | bytes 55304 | tf_op jit(solution)/shard_map/ppermute | solution.py:366
  7.8 0.0 copy-done
  7.8 10.5 %conditional.2 = ((f32[3,4,16,128]{3,2,1,0:T(8,128)S(1)}, f32[3,4,64,128]{3,2,1,0:T(8,128)S(1)}, f32[3,4,64,128]{3,2,1,0:T(8,128)S(1)})) conditional(s32[]{:T(128)} %convert_element_type.4, () %tuple.21, (f32[3,4,3,128]{3,2,1,0:T(4,128)S(1)}, f32[3,4,3,128]{3,2,1,0:T(4,128)S(1)}, f32[3,4,64,128]{3,2,1,0:T(8,128)S(1)}, ...), branch_computations={%region_0.0_spmd, %region_1.0_spmd} | conditional | flops 600000000 | bytes 1147568 | solution.py:464
  7.8 4.0 %collective-permute-start = (f32[3,4,3,128]{3,2,1,0:T(4,128)S(1)}, f32[3,4,3,128]{3,2,1,0:T(4,128)S(1)}, u32[]{:S(2)}, u32[]{:S(2)}) collective-permute-start(f32[3,4,3,128]{3,2,1,0:T(4,128)S(1)} %get-tuple-element.17), channel_id=1, source_target_pairs={{1,2},{2,1},{3,4},{4,3},{5,6},{6,5},{7,8},{8,7},{9,10},{10,9},{11,... | collective-permute-start | bytes 55304 | tf_op jit(solution)/shard_map/cond/branch_1_fun/ppermute | solution.py:366
  11.8 5.2 %collective-permute-start.1 = (f32[3,4,3,128]{3,2,1,0:T(4,128)S(1)}, f32[3,4,3,128]{3,2,1,0:T(4,128)S(1)}, u32[]{:S(2)}, u32[]{:S(2)}) collective-permute-start(f32[3,4,3,128]{3,2,1,0:T(4,128)S(1)} %get-tuple-element.18), channel_id=1, source_target_pairs={{0,1},{1,0},{2,3},{3,2},{4,5},{5,4},{6,7},{7,6},{8,9},{9,8},{10,11... | collective-permute-start | bytes 55304 | tf_op jit(solution)/shard_map/cond/branch_1_fun/ppermute | solution.py:366
  17.0 1.2 %inner.2 = (f32[3,4,64,128]{3,2,1,0:T(8,128)S(1)}, f32[3,4,64,128]{3,2,1,0:T(8,128)S(1)}) custom-call(f32[3,4,64,128]{3,2,1,0:T(8,128)S(1)} %get-tuple-element.16.vel_ref, f32[3,4,64,128]{3,2,1,0:T(8,128)S(1)} %get-tuple-element.19.old_ref), custom_call_target="tpu_custom_call" | custom-call | flops 600000000 | bytes 1000000 | tf_op jit(solution)/shard_map/cond/branch_1_fun/inner/pallas_call | solution.py:405
  18.2 0.0 collective-permute-done.outward_ref
  18.2 0.0 collective-permute-done.1.inward_ref
  18.2 0.1 edges.1
  18.3 1.3 %collective-permute-start.6 = (f32[3,4,3,128]{3,2,1,0:T(4,128)S(1)}, f32[3,4,3,128]{3,2,1,0:T(4,128)S(1)}, u32[]{:S(2)}, u32[]{:S(2)}) collective-permute-start(f32[3,4,3,128]{3,2,1,0:T(4,128)S(1)} %after.3), channel_id=1, source_target_pairs={{0,480},{96,64},{128,96},{160,128},{192,160},{224,192},{256,224},{... | collective-permute-start | bytes 55304 | tf_op jit(solution)/shard_map/ppermute | solution.py:366
  19.6 0.0 collective-permute-done.4.first_ref
  19.6 0.0 collective-permute-done.5.second_ref
  19.6 1.2 %lowest.1 = (f32[3,4,64,128]{3,2,1,0:T(8,128)}, f32[3,4,64,128]{3,2,1,0:T(8,128)}) custom-call(f32[3,4,64,128]{3,2,1,0:T(8,128)S(1)} %get-tuple-element.47.vel_ref, f32[3,4,3,128]{3,2,1,0:T(4,128)S(1)} %collective-permute-done.4.first_ref, f32[3,4,3,128]{3,2,1,0:T(4,128)S(1)} %collective-permute-done.5.second_ref, ...), custom_call_target="tpu_custom_call" | custom-call | tf_op jit(solution)/shard_map/lowest/pallas_call | solution.py:473
  20.8 0.0 collective-permute-done.6.third_ref
  20.8 0.1 outer.1
  (3 shorter events, 0.0 us)
Async XLA Ops:
  0.6 7.1 %copy-start = (f32[3,4,64,128]{3,2,1,0:T(8,128)S(1)}, f32[3,4,64,128]{3,2,1,0:T(8,128)}, u32[]{:S(2)}) copy-start(f32[3,4,64,128]{3,2,1,0:T(8,128)} %param.7) | copy-start | bytes 1179652
  2.1 17.5 %collective-permute-start.4 = (f32[3,4,3,128]{3,2,1,0:T(4,128)S(1)}, f32[3,4,3,128]{3,2,1,0:T(4,128)S(1)}, u32[]{:S(2)}, u32[]{:S(2)}) collective-permute-start(f32[3,4,3,128]{3,2,1,0:T(4,128)S(1)} %get-tuple-element.48), channel_id=1, source_target_pairs={{32,64},{64,32},{480,0},{31,63},{63,95},{95,127},{511,31},{1,33},{... | collective-permute-start | bytes 55304 | tf_op jit(solution)/shard_map/ppermute | solution.py:366
  6.5 13.1 %collective-permute-start.5 = (f32[3,4,3,128]{3,2,1,0:T(4,128)S(1)}, f32[3,4,3,128]{3,2,1,0:T(4,128)S(1)}, u32[]{:S(2)}, u32[]{:S(2)}) collective-permute-start(f32[3,4,3,128]{3,2,1,0:T(4,128)S(1)} %get-tuple-element.49), channel_id=1, source_target_pairs={{0,32},{32,0},{63,31},{95,63},{64,96},{96,128},{128,160},{160,192}... | collective-permute-start | bytes 55304 | tf_op jit(solution)/shard_map/ppermute | solution.py:366
  7.8 10.4 %collective-permute-start = (f32[3,4,3,128]{3,2,1,0:T(4,128)S(1)}, f32[3,4,3,128]{3,2,1,0:T(4,128)S(1)}, u32[]{:S(2)}, u32[]{:S(2)}) collective-permute-start(f32[3,4,3,128]{3,2,1,0:T(4,128)S(1)} %get-tuple-element.17), channel_id=1, source_target_pairs={{1,2},{2,1},{3,4},{4,3},{5,6},{6,5},{7,8},{8,7},{9,10},{10,9},{11,... | collective-permute-start | bytes 55304 | tf_op jit(solution)/shard_map/cond/branch_1_fun/ppermute | solution.py:366
  11.8 6.4 %collective-permute-start.1 = (f32[3,4,3,128]{3,2,1,0:T(4,128)S(1)}, f32[3,4,3,128]{3,2,1,0:T(4,128)S(1)}, u32[]{:S(2)}, u32[]{:S(2)}) collective-permute-start(f32[3,4,3,128]{3,2,1,0:T(4,128)S(1)} %get-tuple-element.18), channel_id=1, source_target_pairs={{0,1},{1,0},{2,3},{3,2},{4,5},{5,4},{6,7},{7,6},{8,9},{9,8},{10,11... | collective-permute-start | bytes 55304 | tf_op jit(solution)/shard_map/cond/branch_1_fun/ppermute | solution.py:366
  18.3 2.5 %collective-permute-start.6 = (f32[3,4,3,128]{3,2,1,0:T(4,128)S(1)}, f32[3,4,3,128]{3,2,1,0:T(4,128)S(1)}, u32[]{:S(2)}, u32[]{:S(2)}) collective-permute-start(f32[3,4,3,128]{3,2,1,0:T(4,128)S(1)} %after.3), channel_id=1, source_target_pairs={{0,480},{96,64},{128,96},{160,128},{192,160},{224,192},{256,224},{... | collective-permute-start | bytes 55304 | tf_op jit(solution)/shard_map/ppermute | solution.py:366

commit v7 on v6

--- a/solution.py
+++ b/solution.py
@@ -86,8 +86,7 @@
     slopes = jnp.where(kind == 0, far1, jnp.where(kind == 2, sign * near1 * touch, 0.0))
     rests = jnp.where(kind == 1, far2, jnp.where(kind == 2, viscosity * near2 * touch, 0.0))
     rests = jnp.where(kind == 3, -0.5 * far1, jnp.where(kind == 4, -0.5 * sign * near1 * touch, rests))
-    high, low = split(jnp.where(slope, slopes, rests))
-    return jnp.concatenate([high, high, low], 0)
+    return jnp.where(slope, slopes, rests)
 
 
 def split(values):
@@ -96,7 +95,7 @@
     return high, low
 
 
-def moments_kernel(vel_ref, held_ref, first_ref, second_ref, third_ref, outward_ref, inward_ref, sems):
+def moments_kernel(vel_ref, held_ref, first_ref, second_ref, third_ref, outward_ref, inward_ref, profiles_ref, sems):
     fields, planes, rows, cols = vel_ref.shape
     lines = planes * rows
     copies = [
@@ -106,6 +105,7 @@
     for i in range(fields):
         for copy in copies[i]:
             copy.start()
+    profiles_ref[...] = outer_table(cols)
     row = lax.broadcasted_iota(jnp.int32, (8, cols), 0)
     cell = lax.broadcasted_iota(jnp.int32, (8, cols), 1)
     away = jnp.where(row < 3, cell, cols - 1 - cell)
@@ -233,20 +233,20 @@
 
 
 def lowest_kernel(
-    vel_ref, first_ref, second_ref, part_ref, base_ref, edges_ref, late_ref,
+    vel_ref, first_ref, second_ref, part_ref, base_ref, edges_ref, profiles_ref, late_ref,
     new_ref, rhs_ref, new_held, rhs_held, sems
 ):
     @pl.when(lax.axis_index("gx") == 0)
     def _():
         finish(
             vel_ref, first_ref, second_ref, None, part_ref, base_ref,
-            lambda i: (edges_ref[i, :, 0:8], edges_ref[i, :, 8:16]),
+            lambda i: (edges_ref[i, :, 0:8], edges_ref[i, :, 8:16]), profiles_ref,
             new_ref, rhs_ref, new_held, rhs_held, sems
         )
 
 
 def outer_kernel(
-    vel_ref, first_ref, second_ref, third_ref, part_ref, base_ref, outward_ref, inward_ref, new_before, rhs_before,
+    vel_ref, first_ref, second_ref, third_ref, part_ref, base_ref, outward_ref, inward_ref, profiles_ref, new_before, rhs_before,
     new_ref, rhs_ref, new_held, rhs_held, below_ref, above_ref, sems
 ):
     @pl.when(lax.axis_index("gx") > 0)
@@ -258,13 +258,13 @@
         set_margins(outward, inward, below_ref, above_ref)
         finish(
             vel_ref, first_ref, second_ref, third_ref, part_ref, base_ref,
-            functools.partial(edge_terms, vel_ref, below_ref, above_ref),
+            functools.partial(edge_terms, vel_ref, below_ref, above_ref), profiles_ref,
             new_ref, rhs_ref, new_held, rhs_held, sems
         )
 
 
 def finish(
-    vel_ref, first_ref, second_ref, third_ref, part_ref, base_ref, edges,
+    vel_ref, first_ref, second_ref, third_ref, part_ref, base_ref, edges, profiles_ref,
     new_ref, rhs_ref, new_held, rhs_held, sems
 ):
     fields, planes, rows, cols = vel_ref.shape
@@ -275,7 +275,8 @@
     third = None if third_ref is None else gathered(third_ref)
     left, right = arrivals(gx, gz, xs, zs, gathered(first_ref), gathered(second_ref), third)
     u_edge = (left[2:3, :lines], right[2:3, :lines])
-    table = outer_table(cols)
+    high, low = split(profiles_ref[...])
+    table = jnp.concatenate([high, high, low], 0)
     tn = (((0,), (0,)), ((), ()))
     copies = []
 
@@ -391,11 +392,11 @@
     result = jax.ShapeDtypeStruct(velocity.shape, f32)
     params = pltpu.CompilerParams(vmem_limit_bytes=32 * 1024 * 1024)
 
-    held, first, second, third, outward, inward = pl.pallas_call(
+    held, first, second, third, outward, inward, profiles = pl.pallas_call(
         moments_kernel,
-        out_shape=(block, halo, halo, halo, halo, halo),
+        out_shape=(block, halo, halo, halo, halo, halo, pltpu.VMEM((16, 2 * cols), f32)),
         in_specs=[pl.BlockSpec(memory_space=pltpu.HBM)],
-        out_specs=(whole,) * 6,
+        out_specs=(whole,) * 7,
         scratch_shapes=[pltpu.SemaphoreType.DMA((fields * planes,))],
         compiler_params=params,
         name="moments",
@@ -481,11 +482,11 @@
         )(*(pltpu.with_memory_space_constraint(x, pltpu.VMEM) for x in arrays), *loose)
 
     before = last(
-        lowest_kernel, (held, first, second, *early[1:], early[0]), (late[0],), [scratch, scratch, sems], name="lowest",
+        lowest_kernel, (held, first, second, *early[1:], early[0], profiles), (late[0],), [scratch, scratch, sems], name="lowest",
     )
     new_velocity, right_side = last(
-        outer_kernel, (held, first, second, third, *late[2:], *late[:2]), before,
-        [scratch, scratch, margins, margins, sems], name="outer", input_output_aliases={8: 0, 9: 1},
+        outer_kernel, (held, first, second, third, *late[2:], *late[:2], profiles), before,
+        [scratch, scratch, margins, margins, sems], name="outer", input_output_aliases={9: 0, 10: 1},
     )
     return new_velocity, right_side
 

time: 21.2 us -> 21.2 us (level)
  no operation moved by 1% of the time
where the time goes in v7:
time: 21.2 us; the launch traced here: 20.9 us
  starting transfers between devices  16.1 us (76%)
  Pallas kernels  3.94 us (19%)
  between operations  0.74 us (3%)
    ppermute x5, starting transfers between devices, permute(): lax.ppermute(values, ('gx', 'gz'), [(a * count + b, c * count + d) for (a...  16.1 us
    pallas_call x1, Pallas kernels, local(): pl.pallas_call(moments_kernel, out_shape=(block, halo, halo, halo, halo,...  1.43 us
    pallas_call x2, Pallas kernels, last(): pl.pallas_call(kernel, out_shape=(result, result), in_specs=[pl.BlockSpec...  1.24 us
    pallas_call x1, Pallas kernels, inner(): pl.pallas_call(inner_kernel, out_shape=(block, block), in_specs=[whole, p...  1.2 us
  transfers between devices with their start and end apart: 5, of which 0 were waited for; matrix products, arithmetic and copies ran while one was open for 0% of the time, Pallas kernels for 12%

profile of v7, /device:TPU:1, one launch (start us, length us, event | category | flops | bytes accessed | tf_op | source)
XLA Modules:
  0.0 20.9 jit_solution(15227958580956825765)
XLA Ops:
  0.6 0.0 copy-start
  0.6 1.4 %moments.1 = (f32[3,4,64,128]{3,2,1,0:T(8,128)S(1)}, f32[3,4,3,128]{3,2,1,0:T(4,128)S(1)}, f32[3,4,3,128]{3,2,1,0:T(4,128)S(1)}, f32[3,4,3,128]{3,2,1,0:T(4,128)...) custom-call(f32[3,4,64,128]{3,2,1,0:T(8,128)} %vel_ref.1), custom_call_target="tpu_custom_call" | custom-call | tf_op jit(solution)/shard_map/moments/pallas_call | solution.py:395
  2.1 4.4 %collective-permute-start.4 = (f32[3,4,3,128]{3,2,1,0:T(4,128)S(1)}, f32[3,4,3,128]{3,2,1,0:T(4,128)S(1)}, u32[]{:S(2)}, u32[]{:S(2)}) collective-permute-start(f32[3,4,3,128]{3,2,1,0:T(4,128)S(1)} %get-tuple-element.49), channel_id=1, source_target_pairs={{32,64},{64,32},{480,0},{31,63},{63,95},{95,127},{511,31},{1,33},{... | collective-permute-start | bytes 55304 | tf_op jit(solution)/shard_map/ppermute | solution.py:367
  6.5 1.3 %collective-permute-start.5 = (f32[3,4,3,128]{3,2,1,0:T(4,128)S(1)}, f32[3,4,3,128]{3,2,1,0:T(4,128)S(1)}, u32[]{:S(2)}, u32[]{:S(2)}) collective-permute-start(f32[3,4,3,128]{3,2,1,0:T(4,128)S(1)} %get-tuple-element.50), channel_id=1, source_target_pairs={{0,32},{32,0},{63,31},{95,63},{64,96},{96,128},{128,160},{160,192}... | collective-permute-start | bytes 55304 | tf_op jit(solution)/shard_map/ppermute | solution.py:367
  7.8 0.0 copy-done
  7.8 10.5 %conditional.2 = ((f32[3,4,16,128]{3,2,1,0:T(8,128)S(1)}, f32[3,4,64,128]{3,2,1,0:T(8,128)S(1)}, f32[3,4,64,128]{3,2,1,0:T(8,128)S(1)})) conditional(s32[]{:T(128)} %convert_element_type.4, () %tuple.21, (f32[3,4,3,128]{3,2,1,0:T(4,128)S(1)}, f32[3,4,3,128]{3,2,1,0:T(4,128)S(1)}, f32[3,4,64,128]{3,2,1,0:T(8,128)S(1)}, ...), branch_computations={%region_0.0_spmd, %region_1.0_spmd} | conditional | flops 600000000 | bytes 1147568 | solution.py:465
  7.8 4.0 %collective-permute-start = (f32[3,4,3,128]{3,2,1,0:T(4,128)S(1)}, f32[3,4,3,128]{3,2,1,0:T(4,128)S(1)}, u32[]{:S(2)}, u32[]{:S(2)}) collective-permute-start(f32[3,4,3,128]{3,2,1,0:T(4,128)S(1)} %get-tuple-element.17), channel_id=1, source_target_pairs={{1,2},{2,1},{3,4},{4,3},{5,6},{6,5},{7,8},{8,7},{9,10},{10,9},{11,... | collective-permute-start | bytes 55304 | tf_op jit(solution)/shard_map/cond/branch_1_fun/ppermute | solution.py:367
  11.8 5.2 %collective-permute-start.1 = (f32[3,4,3,128]{3,2,1,0:T(4,128)S(1)}, f32[3,4,3,128]{3,2,1,0:T(4,128)S(1)}, u32[]{:S(2)}, u32[]{:S(2)}) collective-permute-start(f32[3,4,3,128]{3,2,1,0:T(4,128)S(1)} %get-tuple-element.18), channel_id=1, source_target_pairs={{0,1},{1,0},{2,3},{3,2},{4,5},{5,4},{6,7},{7,6},{8,9},{9,8},{10,11... | collective-permute-start | bytes 55304 | tf_op jit(solution)/shard_map/cond/branch_1_fun/ppermute | solution.py:367
  17.0 1.2 %inner.2 = (f32[3,4,64,128]{3,2,1,0:T(8,128)S(1)}, f32[3,4,64,128]{3,2,1,0:T(8,128)S(1)}) custom-call(f32[3,4,64,128]{3,2,1,0:T(8,128)S(1)} %get-tuple-element.16.vel_ref, f32[3,4,64,128]{3,2,1,0:T(8,128)S(1)} %get-tuple-element.19.old_ref), custom_call_target="tpu_custom_call" | custom-call | flops 600000000 | bytes 1000000 | tf_op jit(solution)/shard_map/cond/branch_1_fun/inner/pallas_call | solution.py:406
  18.2 0.0 collective-permute-done.outward_ref
  18.2 0.0 collective-permute-done.1.inward_ref
  18.2 0.1 edges.1
  18.3 1.3 %collective-permute-start.6 = (f32[3,4,3,128]{3,2,1,0:T(4,128)S(1)}, f32[3,4,3,128]{3,2,1,0:T(4,128)S(1)}, u32[]{:S(2)}, u32[]{:S(2)}) collective-permute-start(f32[3,4,3,128]{3,2,1,0:T(4,128)S(1)} %after.3), channel_id=1, source_target_pairs={{0,480},{96,64},{128,96},{160,128},{192,160},{224,192},{256,224},{... | collective-permute-start | bytes 55304 | tf_op jit(solution)/shard_map/ppermute | solution.py:367
  19.6 0.0 collective-permute-done.4.first_ref
  19.6 0.0 collective-permute-done.5.second_ref
  19.6 1.2 %lowest.1 = (f32[3,4,64,128]{3,2,1,0:T(8,128)}, f32[3,4,64,128]{3,2,1,0:T(8,128)}) custom-call(f32[3,4,64,128]{3,2,1,0:T(8,128)S(1)} %get-tuple-element.48.vel_ref, f32[3,4,3,128]{3,2,1,0:T(4,128)S(1)} %collective-permute-done.4.first_ref, f32[3,4,3,128]{3,2,1,0:T(4,128)S(1)} %collective-permute-done.5.second_ref, ...), custom_call_target="tpu_custom_call" | custom-call | tf_op jit(solution)/shard_map/lowest/pallas_call | solution.py:474
  20.8 0.0 collective-permute-done.6.third_ref
  20.8 0.1 outer.1
  (3 shorter events, 0.0 us)
Async XLA Ops:
  0.6 7.1 %copy-start = (f32[3,4,64,128]{3,2,1,0:T(8,128)S(1)}, f32[3,4,64,128]{3,2,1,0:T(8,128)}, u32[]{:S(2)}) copy-start(f32[3,4,64,128]{3,2,1,0:T(8,128)} %param.7) | copy-start | bytes 1179652
  2.1 17.5 %collective-permute-start.4 = (f32[3,4,3,128]{3,2,1,0:T(4,128)S(1)}, f32[3,4,3,128]{3,2,1,0:T(4,128)S(1)}, u32[]{:S(2)}, u32[]{:S(2)}) collective-permute-start(f32[3,4,3,128]{3,2,1,0:T(4,128)S(1)} %get-tuple-element.49), channel_id=1, source_target_pairs={{32,64},{64,32},{480,0},{31,63},{63,95},{95,127},{511,31},{1,33},{... | collective-permute-start | bytes 55304 | tf_op jit(solution)/shard_map/ppermute | solution.py:367
  6.5 13.1 %collective-permute-start.5 = (f32[3,4,3,128]{3,2,1,0:T(4,128)S(1)}, f32[3,4,3,128]{3,2,1,0:T(4,128)S(1)}, u32[]{:S(2)}, u32[]{:S(2)}) collective-permute-start(f32[3,4,3,128]{3,2,1,0:T(4,128)S(1)} %get-tuple-element.50), channel_id=1, source_target_pairs={{0,32},{32,0},{63,31},{95,63},{64,96},{96,128},{128,160},{160,192}... | collective-permute-start | bytes 55304 | tf_op jit(solution)/shard_map/ppermute | solution.py:367
  7.8 10.4 %collective-permute-start = (f32[3,4,3,128]{3,2,1,0:T(4,128)S(1)}, f32[3,4,3,128]{3,2,1,0:T(4,128)S(1)}, u32[]{:S(2)}, u32[]{:S(2)}) collective-permute-start(f32[3,4,3,128]{3,2,1,0:T(4,128)S(1)} %get-tuple-element.17), channel_id=1, source_target_pairs={{1,2},{2,1},{3,4},{4,3},{5,6},{6,5},{7,8},{8,7},{9,10},{10,9},{11,... | collective-permute-start | bytes 55304 | tf_op jit(solution)/shard_map/cond/branch_1_fun/ppermute | solution.py:367
  11.8 6.4 %collective-permute-start.1 = (f32[3,4,3,128]{3,2,1,0:T(4,128)S(1)}, f32[3,4,3,128]{3,2,1,0:T(4,128)S(1)}, u32[]{:S(2)}, u32[]{:S(2)}) collective-permute-start(f32[3,4,3,128]{3,2,1,0:T(4,128)S(1)} %get-tuple-element.18), channel_id=1, source_target_pairs={{0,1},{1,0},{2,3},{3,2},{4,5},{5,4},{6,7},{7,6},{8,9},{9,8},{10,11... | collective-permute-start | bytes 55304 | tf_op jit(solution)/shard_map/cond/branch_1_fun/ppermute | solution.py:367
  18.3 2.5 %collective-permute-start.6 = (f32[3,4,3,128]{3,2,1,0:T(4,128)S(1)}, f32[3,4,3,128]{3,2,1,0:T(4,128)S(1)}, u32[]{:S(2)}, u32[]{:S(2)}) collective-permute-start(f32[3,4,3,128]{3,2,1,0:T(4,128)S(1)} %after.3), channel_id=1, source_target_pairs={{0,480},{96,64},{128,96},{160,128},{192,160},{224,192},{256,224},{... | collective-permute-start | bytes 55304 | tf_op jit(solution)/shard_map/ppermute | solution.py:367
